TPU v7x, 32 devices: a whole 2x2x4 slice. The times are simulated.
32 devices in a mesh: dp: 2 (over x), expert: 16 (over z, y, core).
Axes of the slice: x: 2, y: 2, z: 4, core: 2. Of those that a mesh axis runs over, the one named last changes fastest.
Arguments:
- tokens: bfloat16 [4096, 2048], P(('dp', 'expert')), may hold values from -6 to 6
- cotangent: bfloat16 [4096, 2048], P(('dp', 'expert')), may hold values from -6 to 6
- segment_ids: int32 [2, 2048], P('dp'), may hold values from 0 to 2, as said below
- routes: int32 [4096, 6], P(('dp', 'expert')), may hold values from 0 to 15, all different within a row; in each aligned block of 128 rows (0 to 127, 128 to 255, ...) at most 72 rows name the same one
- attn_in: bfloat16 [2048, 6144], P(('dp', 'expert')), may hold values from -0.125 to 0.125
- attn_out: bfloat16 [2048, 2048], P(('dp', 'expert')), may hold values from -0.5 to 0.5
- gain_attn: bfloat16 [2048], P(('dp', 'expert')), may hold values from 0.099609375 to 1.8984375
- shared_in: bfloat16 [2048, 5632], P(('dp', 'expert')), may hold values from -0.125 to 0.125
- shared_out: bfloat16 [2816, 2048], P(('dp', 'expert')), may hold values from -0.15625 to 0.15625
- router: bfloat16 [2048, 16], P(('dp', 'expert')), may hold values from -0.0625 to 0.0625
- gain_ffn: bfloat16 [2048], P(('dp', 'expert')), may hold values from 0.099609375 to 1.8984375
- expert_in: bfloat16 [16, 2048, 2816], P('expert', 'dp'), may hold values from -0.125 to 0.125
- expert_out: bfloat16 [16, 1408, 2048], P('expert', 'dp'), may hold values from -0.3125 to 0.3125
Outputs:
- output: bfloat16 [4096, 2048], P(('dp', 'expert'))
- grad_tokens: bfloat16 [4096, 2048], P(('dp', 'expert'))
- grad_attn_in: float32 [2048, 6144], P(('dp', 'expert'))
- grad_attn_out: float32 [2048, 2048], P(('dp', 'expert'))
- grad_gain_attn: float32 [2048], P(('dp', 'expert'))
- grad_shared_in: float32 [2048, 5632], P(('dp', 'expert'))
- grad_shared_out: float32 [2816, 2048], P(('dp', 'expert'))
- grad_router: float32 [2048, 16], P(('dp', 'expert'))
- grad_gain_ffn: float32 [2048], P(('dp', 'expert'))
- grad_expert_in: float32 [16, 2048, 2816], P('expert', 'dp')
- grad_expert_out: float32 [16, 1408, 2048], P('expert', 'dp')
Inputs may be any that keep to these rules, and one draw needn't show every extreme that they name: `routes`: in the rows of one device each expert is named by at most 72 rows, and by exactly 72 rows in some device's rows; a row names 6 different experts. `segment_ids`: ids never fall along a sequence; every sequence holds ids 0, 1 and 2; documents 0 and 2 hold 1 to 127 tokens each.
All inputs are finite; a program needn't handle non-finite values.
Results may differ from a plain program's by a relative error of at most 0.018.
Values may be sent and summed in bfloat16 or wider, within the bound.
No kernel may reach another device: no remote copies, remote signals or barrier semaphores. Data moves between devices by JAX's collectives and lax.ppermute only.
A program may use at most 384 MiB of HBM per device.

v0:
```python
import functools
import math

import jax
import jax.numpy as jnp
from jax import lax
from jax.experimental import pallas as pl
from jax.experimental.pallas import tpu as pltpu
from jax.sharding import PartitionSpec as P

HEADS = 16
HEAD_DIM = 128
TOP = 6


EPS = 1e-06
THETA = 10000.0
NEG = -1e30
HIGHEST = lax.Precision.HIGHEST
BF16 = jnp.bfloat16
F32 = jnp.float32
LOG2E = math.log2(math.e)


def rope_tables(segments):
    length = segments.shape[0]
    places = jnp.arange(length, dtype=jnp.int32)
    starts = jnp.concatenate([jnp.ones((1,), dtype=jnp.bool_), segments[1:] != segments[:-1]])
    first_place = lax.cummax(jnp.where(starts, places, 0), axis=0)
    offset = (places - first_place).astype(jnp.float32)
    half_dim = HEAD_DIM // 2
    freqs = jnp.exp(jnp.arange(half_dim, dtype=jnp.float32) * (-2.0 * math.log(THETA) / HEAD_DIM))
    angles = offset[:, None] * freqs[None, :]
    cos_table, sin_table = jnp.cos(angles), jnp.sin(angles)
    return (
        jnp.concatenate([cos_table, cos_table], axis=1),
        jnp.concatenate([-sin_table, sin_table], axis=1),
        first_place[None, :],
    )


def silu_back(grad_act, gate_part, up_part):
    sigmoid_gate = jax.nn.sigmoid(gate_part)
    gate_grad = grad_act * up_part * sigmoid_gate * (1.0 + gate_part * (1.0 - sigmoid_gate))
    up_grad = grad_act * gate_part * sigmoid_gate
    return jnp.concatenate([gate_grad, up_grad], axis=-1)


def dot(left, right):
    return jnp.dot(left, right, preferred_element_type=F32)


def dot_tn(left, right):
    return lax.dot_general(left, right, (((0,), (0,)), ((), ())), preferred_element_type=F32)


def dot_nt(left, right):
    return lax.dot_general(left, right, (((1,), (1,)), ((), ())), preferred_element_type=F32)


def turn(values, cos_table, sin_table):
    return values * cos_table + pltpu.roll(values, HEAD_DIM // 2, 1) * sin_table


def attend_kernel(sources, block, order_ref, *refs):
    pieces = refs[: sources[-1][-1] + 1]
    weight_ref, cos_ref, sin_ref, start_ref = refs[len(pieces) : len(pieces) + 4]
    o_ref, q_ref, k_ref, v_ref, lse_ref, rows_ref, vt_ref = refs[len(pieces) + 4 :]
    step = pl.program_id(0)
    length = q_ref.shape[0]
    factor = HEAD_DIM ** (-0.5) * LOG2E
    rows = rows_ref.shape[0]

    for n, parts in enumerate(sources):

        @pl.when(step == n)
        def _(parts=parts):
            low = 0
            for part in parts:
                size = pieces[part].shape[0]
                rows_ref[low : low + size, :] = pieces[part][...]
                low += size

    @pl.when(step < len(sources))
    def _():
        qkv = dot(rows_ref[...], weight_ref[...])
        at = pl.ds(pl.multiple_of(order_ref[step] * rows, rows), rows)
        cos_table, sin_table = cos_ref[at, :], sin_ref[at, :]
        q_ref[at, :] = turn(qkv[:, :HEAD_DIM], cos_table, sin_table).astype(BF16)
        k_ref[at, :] = turn(qkv[:, HEAD_DIM : 2 * HEAD_DIM], cos_table, sin_table).astype(BF16)
        value = qkv[:, 2 * HEAD_DIM :]
        v_ref[at, :] = value.astype(BF16)
        vt_ref[:, at] = value.T.astype(BF16)

    for i in range(length // block):

        @pl.when(step == len(sources) + i)
        def _(i=i):
            low, high = i * block, (i + 1) * block
            raw = dot_nt(k_ref[:high, :], q_ref[low:high, :])
            keys = lax.broadcasted_iota(jnp.int32, raw.shape, 0)
            queries = low + lax.broadcasted_iota(jnp.int32, raw.shape, 1)
            allowed = (keys <= queries) & (keys >= start_ref[:, low:high])
            raw = jnp.where(allowed, raw, NEG)
            top = jnp.max(raw, axis=0, keepdims=True)
            shifted = jnp.exp2((raw - top) * factor)
            total = jnp.sum(shifted, axis=0, keepdims=True)
            probs = (shifted * (1.0 / total)).astype(BF16)
            mixed = dot(vt_ref[:, :high], probs)
            o_ref[low:high, :] = mixed.T.astype(BF16)
            lse_ref[:, low:high] = top * factor + jnp.log2(total)


def attend(blocks, order, weight, cos_table, sin_table, first_place):
    pieces, sources = flatten(blocks)
    length = cos_table.shape[0]
    rows = length // len(sources)
    width = weight.shape[0]
    block = min(256, length)
    last = len(sources) - 1
    whole = lambda shape: pl.BlockSpec(shape, lambda i, order: (0, 0))
    head = jax.ShapeDtypeStruct((length, HEAD_DIM), BF16)
    return pl.pallas_call(
        functools.partial(attend_kernel, sources, block),
        out_shape=[head] * 4
        + [jax.ShapeDtypeStruct((1, length), F32), jax.ShapeDtypeStruct((length, width), BF16)],
        grid_spec=pltpu.PrefetchScalarGridSpec(
            num_scalar_prefetch=1,
            grid=(len(sources) + length // block,),
            in_specs=[whole(piece.shape) for piece in pieces]
            + [
                whole(weight.shape),
                whole((length, HEAD_DIM)),
                whole((length, HEAD_DIM)),
                whole((1, length)),
            ],
            out_specs=[whole((length, HEAD_DIM))] * 4
            + [
                whole((1, length)),
                pl.BlockSpec((rows, width), lambda i, order: (jnp.minimum(i, last), 0)),
            ],
            scratch_shapes=[pltpu.VMEM((HEAD_DIM, length), BF16)],
        ),
        compiler_params=pltpu.CompilerParams(vmem_limit_bytes=52 * 2**20),
        name="attend",
    )(order, *pieces, weight, cos_table, sin_table, first_place)


def attend_back_kernel(
    block, rows, order_ref, q_ref, k_ref, v_ref, do_ref, lse_ref, start_ref, cos_ref, sin_ref, out_ref, kt_ref, dq_ref, dk_ref, dv_ref
):
    length = q_ref.shape[0]
    step = pl.program_id(0)
    scale = HEAD_DIM ** (-0.5)
    factor = scale * LOG2E
    count = length // block

    @pl.when(step == 0)
    def _():
        kt_ref[...] = k_ref[...].astype(F32).T.astype(BF16)
        dk_ref[...] = jnp.zeros_like(dk_ref)
        dv_ref[...] = jnp.zeros_like(dv_ref)

    for i in range(count):

        @pl.when(step == i)
        def _(i=i):
            low, high = i * block, (i + 1) * block
            query, grad = q_ref[low:high, :], do_ref[low:high, :]
            raw = dot_nt(k_ref[:high, :], query)
            keys = lax.broadcasted_iota(jnp.int32, raw.shape, 0)
            queries = low + lax.broadcasted_iota(jnp.int32, raw.shape, 1)
            allowed = (keys <= queries) & (keys >= start_ref[:, low:high])
            raw = jnp.where(allowed, raw * factor - lse_ref[:, low:high], NEG)
            probs = jnp.exp2(raw)
            probs_grad = dot_nt(v_ref[:high, :], grad)
            inner = jnp.sum(probs_grad * probs, axis=0, keepdims=True)
            score_grad = (probs * (probs_grad - inner)).astype(BF16)
            dv_ref[:high, :] += dot(probs.astype(BF16), grad)
            dk_ref[:high, :] += dot(score_grad, query)
            dq_ref[low:high, :] = dot(kt_ref[:, :high], score_grad).T

    @pl.when(step == count - 1)
    def _():
        for n in range(length // rows):
            at = pl.ds(pl.multiple_of(order_ref[n] * rows, rows), rows)
            to = slice(n * rows, (n + 1) * rows)
            cos_table, sin_table = cos_ref[at, :], -sin_ref[at, :]
            out_ref[to, :HEAD_DIM] = turn(dq_ref[at, :] * scale, cos_table, sin_table).astype(BF16)
            out_ref[to, HEAD_DIM : 2 * HEAD_DIM] = turn(
                dk_ref[at, :] * scale, cos_table, sin_table
            ).astype(BF16)
            out_ref[to, 2 * HEAD_DIM :] = dv_ref[at, :].astype(BF16)


def attend_back(query, key, value, grad, lse, first_place, cos_table, sin_table, order):
    length = query.shape[0]
    block = min(256, length)
    whole = lambda shape: pl.BlockSpec(shape, lambda i, order: (0, 0))
    head = whole((length, HEAD_DIM))
    return pl.pallas_call(
        functools.partial(attend_back_kernel, block, length // order.shape[0]),
        out_shape=jax.ShapeDtypeStruct((length, 3 * HEAD_DIM), BF16),
        grid_spec=pltpu.PrefetchScalarGridSpec(
            num_scalar_prefetch=1,
            grid=(length // block,),
            in_specs=[head] * 4 + [whole((1, length))] * 2 + [head] * 2,
            out_specs=whole((length, 3 * HEAD_DIM)),
            scratch_shapes=[pltpu.VMEM((HEAD_DIM, length), BF16)]
            + [pltpu.VMEM((length, HEAD_DIM), F32)] * 3,
        ),
        compiler_params=pltpu.CompilerParams(vmem_limit_bytes=48 * 2**20),
        name="attend_back",
    )(order, query, key, value, grad, lse, first_place, cos_table, sin_table)


def dp_gather(value):
    count = lax.axis_size("dp")
    if count == 1:
        return value[None]
    here = lax.axis_index("dp")
    parts = [value] + [
        lax.ppermute(value, "dp", [(i, (i - step) % count) for i in range(count)])
        for step in range(1, count)
    ]
    if count == 2:
        first = here == 0
        return jnp.stack(
            [jnp.where(first, parts[0], parts[1]), jnp.where(first, parts[1], parts[0])]
        )
    whole = jnp.zeros((count,) + value.shape, value.dtype)
    for step, part in enumerate(parts):
        whole = lax.dynamic_update_index_in_dim(whole, part, (here + step) % count, 0)
    return whole


def dp_scatter(value):
    count = lax.axis_size("dp")
    here = lax.axis_index("dp")
    total = lax.dynamic_index_in_dim(value, here, 0, keepdims=False)
    for step in range(1, count):
        block = lax.dynamic_index_in_dim(value, (here + step) % count, 0, keepdims=False)
        got = lax.ppermute(
            block.astype(BF16), "dp", [(i, (i + step) % count) for i in range(count)]
        )
        total = total + got.astype(F32)
    return total


def ring_order():
    pairs = lax.axis_size("expert") // 2
    return list(range(0, pairs, 2)) + list(range(pairs - 1, 0, -2))


def ring_shift(value, step):
    order = ring_order()
    pairs = len(order)
    perm = [
        (order[q] * 2 + c, order[(q + step) % pairs] * 2 + c) for q in range(pairs) for c in range(2)
    ]
    return lax.ppermute(value, "expert", perm)


def core_swap(value):
    count = lax.axis_size("expert")
    return lax.ppermute(value, "expert", [(i, i ^ 1) for i in range(count)])


def ring_offsets():
    half = lax.axis_size("expert") // 4
    return [0] + [o for step in range(1, half) for o in (step, -step)] + [half]


def ring_blocks():
    order = ring_order()
    pairs = len(order)
    table = [[0] * (2 * pairs) for _ in range(2 * pairs)]
    for q in range(pairs):
        for c in range(2):
            for j, offset in enumerate(ring_offsets()):
                for other in range(2):
                    table[order[q] * 2 + c][2 * j + other] = (
                        order[(q - offset) % pairs] * 2 + (c ^ other)
                    )
    return lax.dynamic_index_in_dim(
        jnp.asarray(table, jnp.int32), lax.axis_index("expert"), 0, keepdims=False
    )


def tied(value, *tokens):
    firsts = [lax.slice(t, (0,) * t.ndim, (1,) * t.ndim).reshape(()) for t in tokens]
    token = sum(t.astype(F32) for t in firsts) * 0.0
    return (value.astype(F32) * (1.0 + token)).astype(value.dtype)


def ring_gather(value, gates=None):
    gates = gates or {}
    half_rows = value.shape[0] // 2
    half = lax.axis_size("expert") // 4
    blocks = {}

    def keep(parts, offset):
        blocks[offset] = (parts, [core_swap(part) for part in parts])

    keep([value], 0)
    ahead = back = value
    for step in range(1, half):
        if step in gates:
            token = gates[step](blocks)
            ahead, back = tied(ahead, *token), tied(back, *token)
        ahead, back = ring_shift(ahead, 1), ring_shift(back, -1)
        keep([ahead], step)
        keep([back], -step)
    if half in gates:
        token = gates[half](blocks)
        ahead, back = tied(ahead, *token), tied(back, *token)
    last = [ring_shift(ahead[:half_rows], 1), ring_shift(back[half_rows:], -1)]
    keep(last, half)
    return [parts for offset in ring_offsets() for parts in blocks[offset]]


def flatten(blocks):
    pieces = [piece for parts in blocks for piece in parts]
    sources, n = [], 0
    for parts in blocks:
        sources.append(tuple(range(n, n + len(parts))))
        n += len(parts)
    return pieces, tuple(sources)


def ring_scatter(block, gates=None, marks=None):
    gates = gates or {}
    half = lax.axis_size("expert") // 4
    offsets = ring_offsets()
    spare = {}

    def mine(offset):
        if offset not in spare:
            j = offsets.index(offset)
            spare[offset] = block(2 * j).astype(F32) + core_swap(block(2 * j + 1)).astype(F32)
        return spare[offset]

    far = mine(half).astype(BF16)
    half_rows = far.shape[0] // 2
    ahead = ring_shift(far[:half_rows], 1)
    back = ring_shift(far[half_rows:], -1)
    if marks is not None:
        marks.extend([ahead, back])
    for step in range(half - 1, 0, -1):
        onward, homeward = mine(-step), mine(step)
        if step == half - 1:
            onward = jnp.concatenate(
                [onward[:half_rows] + ahead.astype(F32), onward[half_rows:]], axis=0
            )
            homeward = jnp.concatenate(
                [homeward[:half_rows], homeward[half_rows:] + back.astype(F32)], axis=0
            )
        else:
            onward = onward + ahead.astype(F32)
            homeward = homeward + back.astype(F32)
        if half - step in gates:
            onward, homeward = tied(onward, *gates[half - step]), tied(homeward, *gates[half - step])
        ahead = ring_shift(onward.astype(BF16), 1)
        back = ring_shift(homeward.astype(BF16), -1)
    return mine(0) + ahead.astype(F32) + back.astype(F32)


def chosen(pos_ref, base, window):
    count = pos_ref.shape[-1]
    row = base + lax.broadcasted_iota(jnp.int32, (window, count), 0)
    return row == pos_ref[0]


def dispatch_kernel(sources, widths, window, base_ref, order_ref, pos_ref, gate_ref, *refs):
    outs = refs[-len(widths) - 2 :]
    pieces, blocks, rows_ref, weights_ref = refs[: -len(outs)], outs[:-2], outs[-2], outs[-1]
    step = pl.program_id(0)

    @pl.when(step == 0)
    def _():
        rows_ref[...] = jnp.zeros_like(rows_ref)
        weights_ref[...] = jnp.zeros_like(weights_ref)

    for n, parts in enumerate(sources):

        @pl.when(step == n)
        def _(parts=parts):
            low = 0
            for part in parts:
                size = pieces[part].shape[0]
                left = 0
                for block, wide in zip(blocks, widths):
                    block[low : low + size, :] = pieces[part][:, left : left + wide]
                    left += wide
                low += size

    base = pl.multiple_of(base_ref[step], 16)
    pick = chosen(pos_ref, base, window)
    at = pl.ds(base, window)
    found = dot(pick.astype(F32).astype(BF16), (blocks or pieces)[0][...])
    rows_ref[at, :] = (rows_ref[at, :].astype(F32) + found).astype(BF16)
    weights_ref[at, :] += jnp.sum(jnp.where(pick, gate_ref[0], 0.0), axis=1, keepdims=True)


def dispatch(blocks, widths, packing, order, gates):
    base, pos, _, window, packed = packing
    count, _, rows = pos.shape
    if isinstance(blocks, list):
        pieces, sources = flatten(blocks)
        piece_specs = [pl.BlockSpec(piece.shape, lambda i, base, order: (0, 0)) for piece in pieces]
    else:
        pieces, sources, widths = [blocks], (), []
        piece_specs = [pl.BlockSpec((rows, blocks.shape[1]), lambda i, base, order: (order[i], 0))]
    width = (widths or [pieces[0].shape[1]])[0]
    return pl.pallas_call(
        functools.partial(dispatch_kernel, sources, tuple(widths), window),
        out_shape=[jax.ShapeDtypeStruct((rows * count, wide), BF16) for wide in widths]
        + [
            jax.ShapeDtypeStruct((packed, width), BF16),
            jax.ShapeDtypeStruct((packed, 1), F32),
        ],
        grid_spec=pltpu.PrefetchScalarGridSpec(
            num_scalar_prefetch=2,
            grid=(count,),
            in_specs=[
                pl.BlockSpec((1, 1, rows), lambda i, base, order: (i, 0, 0)),
                pl.BlockSpec((1, 1, rows), lambda i, base, order: (order[i], 0, 0)),
            ]
            + piece_specs,
            out_specs=[
                pl.BlockSpec((rows, wide), lambda i, base, order: (order[i], 0)) for wide in widths
            ]
            + [
                pl.BlockSpec((packed, width), lambda i, base, order: (0, 0)),
                pl.BlockSpec((packed, 1), lambda i, base, order: (0, 0)),
            ],
        ),
        compiler_params=pltpu.CompilerParams(vmem_limit_bytes=52 * 2**20),
        name="dispatch",
    )(base, order, pos, gates, *pieces)


def expert_kernel(ups, total_ref, starts_ref, x_ref, g_ref, gate_ref, *refs):
    parts, refs = refs[:-9], refs[-9:]
    wy_ref, dn_ref, ea_ref, dy_ref, db_ref, dg_ref, up_ref, down_ref, sems = refs
    step = pl.program_id(0)
    rows, hidden = ea_ref.shape
    some = step * rows < total_ref[0]

    @pl.when(step == 0)
    def _():
        copies = []
        for n, part in enumerate(parts):
            at = pl.ds(pl.multiple_of(starts_ref[n], 16), part.shape[0])
            whole = up_ref if n < ups else down_ref
            copies.append(pltpu.make_async_copy(part, whole.at[at, :], sems.at[n]))
        for copy in copies:
            copy.start()
        for copy in copies:
            copy.wait()

    @pl.when(some)
    def _():
        pre = dot(x_ref[...], up_ref[...])
        gate_part, up_part = pre[:, :hidden], pre[:, hidden:]
        sigmoid_gate = 1.0 / (1.0 + jnp.exp(-gate_part))
        silu = gate_part * sigmoid_gate
        act = (silu * up_part).astype(BF16)
        ea_ref[...] = act
        result = dot(act, down_ref[...]).astype(BF16).astype(F32)
        grad = g_ref[...].astype(F32)
        gate = gate_ref[...]
        dg_ref[...] = jnp.sum(grad * result, axis=1, keepdims=True)
        wy_ref[...] = (gate * result).astype(BF16)
        out_grad = (gate * grad).astype(BF16)
        dy_ref[...] = out_grad
        act_grad = dot_nt(out_grad, down_ref[...])
        db_ref[:, :hidden] = (
            act_grad * up_part * sigmoid_gate * (1.0 + gate_part * (1.0 - sigmoid_gate))
        ).astype(BF16)
        db_ref[:, hidden:] = (act_grad * silu).astype(BF16)
        dn_ref[...] = dot_nt(db_ref[...], up_ref[...]).astype(BF16)

    @pl.when(jnp.logical_not(some))
    def _():
        for ref in (wy_ref, dn_ref, ea_ref, dy_ref, db_ref, dg_ref):
            ref[...] = jnp.zeros_like(ref)


def expert(total, rows, grads, gates, ups, downs):
    packed, width = rows.shape
    hidden = sum(part.shape[0] for part, _ in downs)
    tile = 256
    parts = [part for part, _ in ups + downs]
    starts = jnp.stack([start for _, start in ups + downs]).astype(jnp.int32)
    spec = lambda wide: pl.BlockSpec((tile, wide), lambda i, total, starts: (i, 0))
    widths = (width, width, hidden, width, 2 * hidden)
    return pl.pallas_call(
        functools.partial(expert_kernel, len(ups)),
        out_shape=[jax.ShapeDtypeStruct((packed, wide), BF16) for wide in widths]
        + [jax.ShapeDtypeStruct((packed, 1), F32)],
        grid_spec=pltpu.PrefetchScalarGridSpec(
            num_scalar_prefetch=2,
            grid=(packed // tile,),
            in_specs=[spec(width), spec(width), spec(1)]
            + [pl.BlockSpec(memory_space=pl.ANY)] * len(parts),
            out_specs=[spec(wide) for wide in widths] + [spec(1)],
            scratch_shapes=[
                pltpu.VMEM((width, 2 * hidden), BF16),
                pltpu.VMEM((hidden, width), BF16),
                pltpu.SemaphoreType.DMA((len(parts),)),
            ],
        ),
        compiler_params=pltpu.CompilerParams(vmem_limit_bytes=58 * 2**20),
        name="expert",
    )(total, starts, rows, grads, gates, *parts)


def combine_kernel(turned, window, extra, base_ref, order_ref, to_ref, me_ref, pos_ref, rows_ref, dg_ref, act_ref, weight_ref, out_ref):
    mul = dot_nt if turned else dot
    base = pl.multiple_of(base_ref[pl.program_id(0)], 16)
    pick = chosen(pos_ref, base, window)
    at = pl.ds(base, window)
    width = rows_ref.shape[1]
    out_ref[:, :width] = (
        dot_tn(pick.astype(F32).astype(BF16), rows_ref[at, :]) + mul(act_ref[...], weight_ref[...])
    ).astype(BF16)
    if extra:
        count = pick.shape[1]
        line = jnp.sum(jnp.where(pick, dg_ref[at, :], 0.0), axis=0, keepdims=True)
        row = lax.broadcasted_iota(jnp.int32, (count, count), 0)
        lane = lax.broadcasted_iota(jnp.int32, (count, count), 1)
        column = jnp.sum(jnp.where(row == lane, line, 0.0), axis=1, keepdims=True)
        high = column.astype(BF16).astype(F32)
        lane = lax.broadcasted_iota(jnp.int32, (count, extra), 1)
        out_ref[:, width:] = jnp.where(
            lane == me_ref[0], high, jnp.where(lane == me_ref[0] + extra // 2, column - high, 0.0)
        ).astype(BF16)


def combine(packing, order, to, me, rows, dg, act, weight, turned, extra):
    base, pos, _, window, packed = packing
    blocks, _, count = pos.shape
    width = rows.shape[-1]
    whole = lambda ref: pl.BlockSpec(ref.shape, lambda i, *_: (0, 0))
    return pl.pallas_call(
        functools.partial(combine_kernel, turned, window, extra),
        out_shape=jax.ShapeDtypeStruct((blocks * count, width + extra), BF16),
        grid_spec=pltpu.PrefetchScalarGridSpec(
            num_scalar_prefetch=4,
            grid=(blocks,),
            in_specs=[
                pl.BlockSpec((1, 1, count), lambda i, *_: (i, 0, 0)),
                whole(rows),
                whole(dg),
                pl.BlockSpec((count, act.shape[1]), lambda i, base, order, to, me: (order[i], 0)),
                whole(weight),
            ],
            out_specs=pl.BlockSpec(
                (count, width + extra), lambda i, base, order, to, me: (to[i], 0)
            ),
        ),
        compiler_params=pltpu.CompilerParams(vmem_limit_bytes=40 * 2**20),
        name="combine",
    )(base, order, to, me.reshape(1), pos, rows, dg, act, weight)


def gather_all(value):
    return lax.all_gather(value, "expert", axis=0, tiled=True)


def swap(value):
    return lax.all_to_all(value, "expert", split_axis=0, concat_axis=0, tiled=True)


def per_device(
    tokens,
    cotangent,
    segment_ids,
    routes,
    attn_in,
    attn_out,
    gain_attn,
    shared_in,
    shared_out,
    router,
    gain_ffn,
    expert_in,
    expert_out,
):
    n_dp, n_e = lax.axis_size("dp"), lax.axis_size("expert")
    me = lax.axis_index("expert")
    count, width = tokens.shape
    segments = segment_ids[0]
    length = segments.shape[0]
    rows = attn_in.shape[0]
    capacity = min(count, 3 * TOP * count // (2 * n_e))
    shared_rows = shared_out.shape[0]
    shared_width = shared_rows * n_dp
    expert_width = expert_out.shape[1] * n_dp

    order = ring_blocks()
    steady = jnp.arange(n_e, dtype=jnp.int32)
    hidden_in = tokens.astype(F32)
    inverse_one = lax.rsqrt(jnp.mean(hidden_in * hidden_in, axis=-1, keepdims=True) + EPS)
    normed_one = hidden_in * inverse_one
    gain_rows = gain_attn.astype(F32)[:, None]
    head_w = []

    def head_sent(blocks):
        own = (attn_in.astype(F32) * tied(gain_rows, blocks[0][1][0])).astype(BF16)
        own = own.reshape(rows, 3, n_e, HEAD_DIM).transpose(2, 0, 1, 3)
        head_w.append(swap(own.reshape(n_e, rows, 3 * HEAD_DIM)))
        return head_w[0]

    def head_whole(blocks):
        head_w.append(dp_gather(head_w[0]).reshape(width, 3 * HEAD_DIM))
        return head_w[1]

    here = lax.axis_index("dp")

    def spread(shard, chunks):
        while shard.shape[0] % (16 * chunks):
            chunks -= 1
        size = shard.shape[0] // chunks
        parts = [[(shard, here * shard.shape[0])]]
        for j in range(chunks):
            parts.append([])
            for step in range(1, n_dp):
                got = lax.ppermute(
                    shard[j * size : (j + 1) * size],
                    "dp",
                    [(i, (i - step) % n_dp) for i in range(n_dp)],
                )
                parts[-1].append((got, (here + step) % n_dp * shard.shape[0] + j * size))
        return parts

    up_parts = spread(expert_in[0], max(1, min(4, expert_in.shape[1] // 256)))
    down_parts = spread(expert_out[0], 2)
    first = lambda parts: [part for part, _ in parts]
    up_tokens = [first(parts) for parts in up_parts[1:]] + [[]] * 4

    small = jnp.concatenate([router, gain_ffn[:, None]], axis=1)
    small = dp_gather(small).reshape(-1, n_e + 1)
    extra_rows = 32
    extra = jnp.concatenate([small.T, routes.T.astype(BF16)], axis=0)
    extra = jnp.pad(extra, ((0, extra_rows - extra.shape[0]), (0, 0)))
    extra = jnp.broadcast_to(extra, (n_e,) + extra.shape)
    cos_table, sin_table, first_place = rope_tables(segments)
    share_w = shared_in.reshape(rows, 2, n_dp, n_e, shared_rows).transpose(3, 0, 1, 2, 4)
    share_w = share_w.reshape(n_e, rows, 2 * shared_width)

    half = n_e // 4
    norm_blocks = ring_gather(
        normed_one.astype(BF16),
        {
            half - 1: lambda blocks: [head_sent(blocks)],
            half: lambda blocks: [head_whole(blocks), cos_table, sin_table, extra, share_w]
            + up_tokens[0],
        },
    )
    head_sent_w, head_w = head_w

    head_out, query, key, value, lse, norm_all = attend(
        norm_blocks, order, head_w, cos_table, sin_table, first_place
    )
    mixed = jnp.concatenate([head_out.reshape(n_e, count, HEAD_DIM), extra], axis=1)
    share_w = swap(tied(share_w, head_sent_w))
    mixed = swap(tied(mixed, share_w, *up_tokens[1]))
    small = mixed[:, count:]
    mixed = mixed[:, :count].transpose(1, 0, 2).reshape(count, n_dp, n_e, rows)
    mixed = mixed.transpose(0, 2, 1, 3).reshape(count, width)
    proj_all = gather_all(dp_gather(attn_out).reshape(n_dp * rows, width))
    routes_all = small[:, n_e + 1 : n_e + 1 + TOP].astype(F32)
    small = small[:, : n_e + 1].reshape(n_e, n_e + 1, n_dp, rows).transpose(1, 2, 0, 3)
    small = small.reshape(n_e + 1, width)
    router_full = small[:n_e]
    gain_second = small[n_e].astype(F32)
    cot_all = gather_all(cotangent)

    share_sent = share_w
    share_w = dp_gather(share_w).reshape(width, 2 * shared_width)
    share_out = dp_gather(shared_out).reshape(shared_width, width)
    resid = hidden_in + dot(mixed, proj_all)
    if up_tokens[2]:
        resid = tied(resid, *up_tokens[2])

    inverse_two = lax.rsqrt(jnp.mean(resid * resid, axis=-1, keepdims=True) + EPS)
    normed_two = resid * inverse_two
    norm_two = (normed_two * gain_second).astype(BF16)
    logits = dot_nt(norm_two, router_full)
    picked = jnp.any(routes[:, :, None] == jnp.arange(n_e)[None, None, :], axis=1)
    chosen = jnp.where(picked, logits, NEG)
    chosen = jnp.where(picked, jnp.exp(chosen - jnp.max(chosen, axis=-1, keepdims=True)), 0.0)
    gates = chosen / jnp.sum(chosen, axis=-1, keepdims=True)
    gate_high = gates.astype(BF16)
    gate_low = (gates - gate_high.astype(F32)).astype(BF16)
    blank = jnp.zeros((count, 128 - 2 * n_e), BF16)
    payload = jnp.concatenate([norm_two, gate_high, gate_low, blank], axis=1)
    norm_blocks = ring_gather(
        payload,
        {
            half - 1: lambda blocks: [share_sent] + up_tokens[3],
            half: lambda blocks: first(down_parts[1]) + [share_sent],
        },
    )

    named = jnp.any(routes_all == me.astype(F32), axis=1)
    named = jnp.take(named, order, axis=0)
    ranking = jnp.cumsum(named.astype(jnp.int32), axis=1)
    ends = jnp.cumsum(ranking[:, -1])
    begins = ends - ranking[:, -1]
    pos = jnp.where(named, begins[:, None] + ranking - 1, -1)[:, None, :]
    window = -(-(capacity + 15) // 16) * 16
    packed = -(-(n_e * capacity + 32) // 256) * 256
    packing = (begins // 16 * 16, pos, ends[-1:], window, packed)
    norm_two_all, payload, arrived, _ = dispatch(
        norm_blocks, [width, 128], packing, order, jnp.zeros((n_e, 1, count), F32)
    )
    mine = jnp.arange(n_e) == me
    gate_all = payload[:, : 2 * n_e].astype(F32).reshape(length, 2, n_e)
    gate_all = jnp.sum(jnp.where(mine, gate_all, 0.0), axis=(1, 2)).reshape(n_e, 1, count)
    cot_rows, gate_rows = dispatch(cot_all, None, packing, order, gate_all)
    weighted, row_grad, expert_act, route_grad, pre_grad, gate_grad = expert(
        packing[2],
        arrived,
        cot_rows,
        gate_rows,
        [part for parts in up_parts for part in parts],
        [part for parts in down_parts for part in parts],
    )

    shared_pre = dot(norm_two_all, share_w)
    shared_act = (
        jax.nn.silu(shared_pre[:, :shared_width]) * shared_pre[:, shared_width:]
    ).astype(BF16)
    shared_act_grad = dot_nt(cot_all, share_out)
    shared_pre_grad = silu_back(
        shared_act_grad, shared_pre[:, :shared_width], shared_pre[:, shared_width:]
    ).astype(BF16)
    norm_two_part = combine(
        packing, order, steady, me, row_grad, gate_grad, shared_pre_grad, share_w, True, 128
    )
    marks = []
    norm_two_grad = ring_scatter(
        lambda n: norm_two_part[n * count : (n + 1) * count], None, marks
    )
    gate_grad = norm_two_grad[:, width : width + n_e] + norm_two_grad[:, width + 64 : width + 64 + n_e]
    norm_two_grad = norm_two_grad[:, :width]
    out_part = combine(
        packing, order, order, me, weighted, gate_rows, shared_act, share_out, False, 0
    )
    routed_out = lax.psum_scatter(out_part, "expert", scatter_dimension=0, tiled=True)

    def shard_grads(left, right, chunks):
        size = left.shape[1] // n_dp
        part = size // chunks
        cut = lambda start, wide: tied(lax.dynamic_slice_in_dim(left, start, wide, 1), *marks)
        got = [
            [
                lax.ppermute(
                    dot_tn(cut((here + step) % n_dp * size + j * part, part), right).astype(BF16),
                    "dp",
                    [(i, (i + step) % n_dp) for i in range(n_dp)],
                )
                for step in range(1, n_dp)
            ]
            for j in range(chunks)
        ]
        return dot_tn(cut(here * size, size), right), got

    def shard_sum(own, got, tokens):
        part = own.shape[0] // len(got)
        own = own[None]
        for j, (parts, token) in enumerate(zip(got, tokens)):
            block = sum(tied(p.astype(F32), token) for p in parts)[None]
            block = own[:, j * part : (j + 1) * part] + block
            own = lax.dynamic_update_slice_in_dim(own, block, j * part, 1)
        return own

    down_own, down_got = shard_grads(expert_act, route_grad, 2)
    up_own, up_got = shard_grads(arrived, pre_grad, len(up_parts) - 1)

    share_out_grad = dp_scatter(dot_tn(shared_act, cot_all).reshape(n_dp, shared_rows, width))
    share_in_grad = dot_tn(norm_two_all, shared_pre_grad)
    share_in_grad = dp_scatter(share_in_grad.reshape(n_dp, n_e, rows, 2 * shared_width))
    share_in_grad = swap(share_in_grad.astype(BF16)).astype(F32)
    share_in_grad = (
        share_in_grad.reshape(n_e, rows, 2, n_dp, shared_rows)
        .transpose(1, 2, 3, 0, 4)
        .reshape(rows, -1)
    )

    logit_grad = gates * (gate_grad - jnp.sum(gates * gate_grad, axis=-1, keepdims=True))
    router_grad = jnp.dot(
        logit_grad.T, norm_two.astype(F32), precision=HIGHEST, preferred_element_type=F32
    )
    norm_two_grad = norm_two_grad + jnp.dot(
        logit_grad, router_full.astype(F32), precision=HIGHEST, preferred_element_type=F32
    )
    gain_two_grad = jnp.sum(norm_two_grad * normed_two, axis=0)
    upstream = cotangent.astype(F32)
    scaled_two = norm_two_grad * gain_second
    resid_grad = upstream + inverse_two * (
        scaled_two - normed_two * jnp.mean(scaled_two * normed_two, axis=-1, keepdims=True)
    )
    small_grad = jnp.concatenate([router_grad, gain_two_grad[None]], axis=0)

    branch_cot = resid_grad.astype(BF16)
    proj_grad = dot_tn(mixed, branch_cot).astype(BF16)
    mixed_grad = tied(dot_nt(branch_cot, proj_all), proj_grad, *down_got[0]).astype(BF16)
    mixed_grad = mixed_grad.reshape(count, n_e, n_dp, rows).transpose(0, 2, 1, 3)
    mixed_grad = swap(mixed_grad.reshape(count, n_e, HEAD_DIM).transpose(1, 0, 2))
    mixed_grad = mixed_grad.reshape(length, HEAD_DIM)
    proj_grad = lax.psum_scatter(proj_grad, "expert", scatter_dimension=0, tiled=True)
    attn_out_grad = dp_scatter(proj_grad.astype(F32).reshape(n_dp, rows, width))
    qkv_grad = attend_back(
        query, key, value, mixed_grad, lse, first_place, cos_table, sin_table, order
    )
    small_grad = tied(small_grad, qkv_grad).reshape(n_e + 1, n_dp * n_e, rows).transpose(1, 0, 2)
    small_grad = lax.all_to_all(
        small_grad, ("dp", "expert"), split_axis=0, concat_axis=0, tiled=True
    )
    small_grad = jnp.sum(small_grad, axis=0)
    norm_one_part = dot_nt(qkv_grad, head_w).astype(BF16)
    scaled_one = ring_scatter(
        lambda n: norm_one_part[n * count : (n + 1) * count],
        {1: down_got[1], half - 1: up_got[0]},
    )
    expert_out_grad = shard_sum(down_own, down_got, [mixed_grad, scaled_one])
    expert_in_grad = shard_sum(up_own, up_got, ([qkv_grad] + [scaled_one] * 3)[: len(up_got)])
    input_grad = resid_grad + inverse_one * (
        scaled_one - normed_one * jnp.mean(scaled_one * normed_one, axis=-1, keepdims=True)
    )
    head_grad = dot_tn(norm_all, qkv_grad).reshape(n_dp, n_e, rows, 3 * HEAD_DIM)
    head_grad = swap(dp_scatter(head_grad).astype(BF16)).astype(F32)
    head_grad = (
        head_grad.reshape(n_e, rows, 3, HEAD_DIM).transpose(1, 2, 0, 3).reshape(rows, 3 * width)
    )
    gain_attn_grad = jnp.sum(head_grad * attn_in.astype(F32), axis=1)
    attn_in_grad = head_grad * gain_rows
    return (
        (resid + routed_out.astype(F32)).astype(BF16),
        input_grad.astype(BF16),
        attn_in_grad,
        attn_out_grad,
        gain_attn_grad,
        share_in_grad,
        share_out_grad,
        small_grad[:n_e].T,
        small_grad[n_e],
        expert_in_grad,
        expert_out_grad,
    )


def solution(mesh):
    return jax.shard_map(
        per_device,
        mesh=mesh,
        in_specs=(
            P(("dp", "expert"), None),
            P(("dp", "expert"), None),
            P("dp", None),
            P(("dp", "expert"), None),
            P(("dp", "expert"), None),
            P(("dp", "expert"), None),
            P(("dp", "expert")),
            P(("dp", "expert"), None),
            P(("dp", "expert"), None),
            P(("dp", "expert"), None),
            P(("dp", "expert")),
            P("expert", "dp", None),
            P("expert", "dp", None),
        ),
        out_specs=(
            P(("dp", "expert"), None),
            P(("dp", "expert"), None),
            P(("dp", "expert"), None),
            P(("dp", "expert"), None),
            P(("dp", "expert")),
            P(("dp", "expert"), None),
            P(("dp", "expert"), None),
            P(("dp", "expert"), None),
            P(("dp", "expert")),
            P("expert", "dp", None),
            P("expert", "dp", None),
        ),
        check_vma=False,
    )
```

profile of v0, /device:TPU:0, one launch (start us, length us, event | category | flops | bytes accessed | tf_op | source)
XLA Modules:
  0.0 907.0 jit_solution(3377206758983063599)
XLA Ops:
  63.9 30.1 %collective-permute-done.15.refs_1_ = bf16[256,2816]{1,0:T(8,128)(2,1)} collective-permute-done((bf16[256,2816]{1,0:T(8,128)(2,1)}, bf16[256,2816]{1,0:T(8,128)(2,1)}, u32[]{:S(2)}, u32[]{:S(2)}) %collective-permute-start.15) | collective-permute-done | bytes 1441824 | tf_op jit(solution)/shard_map/ppermute | solution.py:630
  111.0 14.5 %collective-permute-done.13 = bf16[16,64,384]{2,1,0:T(8,128)(2,1)S(1)} collective-permute-done((bf16[16,64,384]{2,1,0:T(8,128)(2,1)}, bf16[16,64,384]{2,1,0:T(8,128)(2,1)S(1)}, u32[]{:S(2)}, u32[]{:S(2)}) %collective-permute-start.13) | collective-permute-done | bytes 786464 | tf_op jit(solution)/shard_map/ppermute | solution.py:223
  150.2 8.2 collective-permute-done.16.refs_14_
  165.8 29.2 %attend.1 = (bf16[2048,128]{1,0:T(8,128)(2,1)S(1)}, bf16[2048,128]{1,0:T(8,128)(2,1)}, bf16[2048,128]{1,0:T(8,128)(2,1)}, bf16[2048,128]{1,0:T(8,128)(2,1)}, f32...) custom-call(s32[16]{0:T(128)S(1)} %fusion.69.order_ref.to_ref, bf16[128,2048]{1,0:T(8,128)(2,1)} %fusion.18.refs_0_, ...), custom_call_target="tpu_custom_call" | custom-call | tf_op jit(solution)/shard_map/attend/pallas_call | solution.py:123
  230.9 15.4 %collective-permute-done.37.refs_6_ = bf16[352,2048]{1,0:T(8,128)(2,1)} collective-permute-done((bf16[352,2048]{1,0:T(8,128)(2,1)}, bf16[352,2048]{1,0:T(8,128)(2,1)}, u32[]{:S(2)}, u32[]{:S(2)}) %collective-permute-start.37) | collective-permute-done | bytes 1441824 | tf_op jit(solution)/shard_map/ppermute | solution.py:630
  247.5 29.7 %collective-permute-done.32.refs_4_ = bf16[256,2816]{1,0:T(8,128)(2,1)} collective-permute-done((bf16[256,2816]{1,0:T(8,128)(2,1)}, bf16[256,2816]{1,0:T(8,128)(2,1)}, u32[]{:S(2)}, u32[]{:S(2)}) %collective-permute-start.32) | collective-permute-done | bytes 1441824 | tf_op jit(solution)/shard_map/ppermute | solution.py:630
  283.1 10.5 %collective-permute-done.43 = bf16[16,64,352]{2,1,0:T(8,128)(2,1)} collective-permute-done((bf16[16,64,352]{2,1,0:T(8,128)(2,1)}, bf16[16,64,352]{2,1,0:T(8,128)(2,1)}, u32[]{:S(2)}, u32[]{:S(2)}) %collective-permute-start.43) | collective-permute-done | bytes 720928 | tf_op jit(solution)/shard_map/ppermute | solution.py:223
  299.9 11.6 %collective-permute-done.28.refs_6_ = bf16[128,2176]{1,0:T(8,128)(2,1)S(1)} collective-permute-done((bf16[128,2176]{1,0:T(8,128)(2,1)}, bf16[128,2176]{1,0:T(8,128)(2,1)S(1)}, u32[]{:S(2)}, u32[]{:S(2)}) %collective-permute-start.28) | collective-permute-done | bytes 557088 | tf_op jit(solution)/shard_map/ppermute | solution.py:261
  315.4 10.0 %collective-permute-done.33.refs_10_ = bf16[128,2176]{1,0:T(8,128)(2,1)S(1)} collective-permute-done((bf16[128,2176]{1,0:T(8,128)(2,1)S(1)}, bf16[128,2176]{1,0:T(8,128)(2,1)S(1)}, u32[]{:S(2)}, u32[]{:S(2)}) %collective-permute-start.33) | collective-permute-done | bytes 557088 | tf_op jit(solution)/shard_map/ppermute | solution.py:261
  339.3 14.1 %dispatch.2 = (bf16[2048,2048]{1,0:T(8,128)(2,1)}, bf16[2048,128]{1,0:T(8,128)(2,1)S(1)}, bf16[1280,2048]{1,0:T(8,128)(2,1)}, f32[1280,1]{1,0:T(8,128)}) custom-call(s32[16]{0:T(128)S(1)} %fusion.68.base_ref, s32[16]{0:T(128)S(1)} %fusion.69.order_ref.to_ref, s32[16,1,128]{2,1,0:T(1,128)S(1)} %fusion.54.pos_ref, ...), custom_call_target="tpu_custom_call" | custom-call | tf_op jit(solution)/shard_map/dispatch/pallas_call | solution.py:415
  353.3 8.6 fusion.78
  362.2 14.7 %dispatch.3 = (bf16[1280,2048]{1,0:T(8,128)(2,1)}, f32[1280,1]{1,0:T(8,128)S(1)}) custom-call(s32[16]{0:T(128)S(1)} %fusion.68.base_ref, s32[16]{0:T(128)S(1)} %fusion.69.order_ref.to_ref, s32[16,1,128]{2,1,0:T(1,128)S(1)} %fusion.54.pos_ref, f32[16,1,128]{2,1,0:T(1,128)S(1)} %bitcast.221, bf16[2048,2048]{1,0:T(8,128)(2,1)} %all-gather.5.cloned.1.call-done.refs_0_), custom_call_target="tpu_custom_call" | custom-call | tf_op jit(solution)/shard_map/dispatch/pallas_call | solution.py:415
  383.5 54.7 %expert.1 = (bf16[1280,2048]{1,0:T(8,128)(2,1)}, bf16[1280,2048]{1,0:T(8,128)(2,1)}, bf16[1280,1408]{1,0:T(8,128)(2,1)}, bf16[1280,2048]{1,0:T(8,128)(2,1)}, bf1...) custom-call(s32[1]{0:T(128)} %bitcast.38.total_ref, s32[8]{0:T(128)} %stack.89.starts_ref, ...), custom_call_target="tpu_custom_call" | custom-call | tf_op jit(solution)/shard_map/expert/pallas_call | solution.py:498
  441.7 13.9 %combine.3 = bf16[2048,2176]{1,0:T(8,128)(2,1)} custom-call(s32[16]{0:T(128)S(1)} %fusion.68.base_ref, s32[16]{0:T(128)S(1)} %fusion.69.order_ref.to_ref, s32[16]{0:T(128)S(1)} %iota.41.to_ref, s32[1]{0:T(128)} %bitcast.35.me_ref, s32[16,1,128]{2,1,0:T(1,128)S(1)} %fusion.54.pos_ref, bf16[1280,2048]{1,0:T(8,128)(2,1)S(1)} %copy-done.5, ...), custom_call_target="tpu_custom_call" | custom-call | tf_op jit(solution)/shard_map/combine/pallas_call | solution.py:546
  460.0 8.8 collective-permute-start.49
  472.5 11.0 %combine.2 = bf16[2048,2048]{1,0:T(8,128)(2,1)} custom-call(s32[16]{0:T(128)S(1)} %fusion.68.base_ref, s32[16]{0:T(128)S(1)} %fusion.69.order_ref.to_ref, s32[16]{0:T(128)S(1)} %fusion.69.order_ref.to_ref, s32[1]{0:T(128)} %bitcast.35.me_ref, s32[16,1,128]{2,1,0:T(1,128)S(1)} %fusion.54.pos_ref, bf16[1280,2048]{1,0:T(8,128)(2,1)S(1)} %copy-done.4, ...), custom_call_target="tpu_custom_call" | custom-call | tf_op jit(solution)/shard_map/combine/pallas_call | solution.py:546
  499.8 9.3 %collective-permute-done.51 = bf16[128,2176]{1,0:T(8,128)(2,1)S(1)} collective-permute-done((bf16[128,2176]{1,0:T(8,128)(2,1)S(1)}, bf16[128,2176]{1,0:T(8,128)(2,1)S(1)}, u32[]{:S(2)}, u32[]{:S(2)}) %collective-permute-start.51) | collective-permute-done | bytes 557088 | tf_op jit(solution)/shard_map/ppermute | solution.py:261
  513.8 18.2 %collective-permute-done.52 = bf16[128,2176]{1,0:T(8,128)(2,1)S(1)} collective-permute-done((bf16[128,2176]{1,0:T(8,128)(2,1)S(1)}, bf16[128,2176]{1,0:T(8,128)(2,1)S(1)}, u32[]{:S(2)}, u32[]{:S(2)}) %collective-permute-start.52) | collective-permute-done | bytes 557088 | tf_op jit(solution)/shard_map/ppermute | solution.py:261
  532.0 9.7 %collective-permute-start.57 = (bf16[64,2176]{1,0:T(8,128)(2,1)S(1)}, bf16[64,2176]{1,0:T(8,128)(2,1)S(1)}, u32[]{:S(2)}, u32[]{:S(2)}) collective-permute-start(bf16[64,2176]{1,0:T(8,128)(2,1)S(1)} %get-tuple-element.102), channel_id=1, source_target_pairs={{0,2},{1,3},{4,0},{5,1},{8,4},{9,5},{12,8},{13,9},{14,12},{15,13},... | collective-permute-start | bytes 835592 | tf_op jit(solution)/shard_map/ppermute | solution.py:261
  543.3 11.0 %collective-permute-done.57 = bf16[64,2176]{1,0:T(8,128)(2,1)S(1)} collective-permute-done((bf16[64,2176]{1,0:T(8,128)(2,1)S(1)}, bf16[64,2176]{1,0:T(8,128)(2,1)S(1)}, u32[]{:S(2)}, u32[]{:S(2)}) %collective-permute-start.57) | collective-permute-done | bytes 278560 | tf_op jit(solution)/shard_map/ppermute | solution.py:261
  563.1 8.3 collective-permute-done.58
  575.5 10.8 %convolution_bitcast_fusion = f32[1,1024,2816]{2,1,0:T(8,128)} fusion(bf16[1280,2816]{1,0:T(8,128)(2,1)S(1)} %bitcast.223, f32[]{:T(128)} %bitcast.64, bf16[1280,2048]{1,0:T(8,128)(2,1)S(1)} %bitcast.230, s32[]{:T(128)S(6)} %select_n.234), kind=kOutput, calls=%fused_computation.3 | convolution fusion | flops 7385907200 | bytes 21364744 | tf_op jit(solution)/shard_map/dot_general | solution.py:54
  595.0 14.0 %collective-permute-done.53 = bf16[128,2176]{1,0:T(8,128)(2,1)S(1)} collective-permute-done((bf16[128,2176]{1,0:T(8,128)(2,1)S(1)}, bf16[128,2176]{1,0:T(8,128)(2,1)S(1)}, u32[]{:S(2)}, u32[]{:S(2)}) %collective-permute-start.53) | collective-permute-done | bytes 557088 | tf_op jit(solution)/shard_map/ppermute | solution.py:261
  633.7 7.6 all-to-all-start.3
  649.5 9.2 %convolution_bitcast_fusion.1 = f32[1,704,2048]{2,1,0:T(8,128)} fusion(bf16[1280,2048]{1,0:T(8,128)(2,1)} %get-tuple-element.41, f32[]{:T(128)} %bitcast.64, bf16[1280,1408]{1,0:T(8,128)(2,1)S(1)} %copy-done.64, s32[]{:T(128)S(6)} %select_n.238), kind=kOutput, calls=%fused_computation.10 | convolution fusion | flops 3693690880 | bytes 12976136 | tf_op jit(solution)/shard_map/dot_general | solution.py:54
  668.9 10.8 %attend_back.1 = bf16[2048,384]{1,0:T(8,128)(2,1)S(1)} custom-call(s32[16]{0:T(128)S(1)} %fusion.69.order_ref.to_ref, bf16[2048,128]{1,0:T(8,128)(2,1)S(1)} %copy-done.11, bf16[2048,128]{1,0:T(8,128)(2,1)S(1)} %copy-done.12, bf16[2048,128]{1,0:T(8,128)(2,1)S(1)} %copy-done.13, bf16[2048,128]{1,0:T(8,128)(2,1)S(1)} %bitcast.216, ...), custom_call_target="tpu_custom_call" | custom-call | tf_op jit(solution)/shard_map/attend_back/pallas_call | solution.py:201
  742.5 8.8 fusion.79
  766.4 12.6 %collective-permute-start.76 = (bf16[64,2048]{1,0:T(8,128)(2,1)}, bf16[64,2048]{1,0:T(8,128)(2,1)S(1)}, u32[]{:S(2)}, u32[]{:S(2)}) collective-permute-start(bf16[64,2048]{1,0:T(8,128)(2,1)} %get-tuple-element.104), channel_id=1, source_target_pairs={{0,2},{1,3},{4,0},{5,1},{8,4},{9,5},{12,8},{13,9},{14,12},{15,13},... | collective-permute-start | bytes 786440 | tf_op jit(solution)/shard_map/ppermute | solution.py:261
  793.8 11.3 %collective-permute-done.80 = bf16[16,64,384]{2,1,0:T(8,128)(2,1)S(1)} collective-permute-done((bf16[16,64,384]{2,1,0:T(8,128)(2,1)S(1)}, bf16[16,64,384]{2,1,0:T(8,128)(2,1)S(1)}, u32[]{:S(2)}, u32[]{:S(2)}) %collective-permute-start.80) | collective-permute-done | bytes 786464 | tf_op jit(solution)/shard_map/ppermute | solution.py:243
  809.9 8.3 all-to-all-start.4
  832.7 12.0 %all-to-all-done.4 = bf16[16,64,384]{2,1,0:T(8,128)(2,1)S(1)} async-done(((bf16[16,64,384]{2,1,0:T(8,128)(2,1)}), bf16[16,64,384]{2,1,0:T(8,128)(2,1)S(1)}, u32[]{:S(2)}, u32[]{:S(2)}) %all-to-all-start.4) | async-done | bytes 786464 | tf_op jit(solution)/shard_map/all_to_all | solution.py:573
  863.0 19.5 %collective-permute-done.85 = bf16[256,2816]{1,0:T(8,128)(2,1)S(1)} collective-permute-done((bf16[256,2816]{1,0:T(8,128)(2,1)S(1)}, bf16[256,2816]{1,0:T(8,128)(2,1)S(1)}, u32[]{:S(2)}, u32[]{:S(2)}) %collective-permute-start.85) | collective-permute-done | bytes 1441824 | tf_op jit(solution)/shard_map/ppermute | solution.py:761
  (542 shorter events, 409.0 us)
Async XLA Ops:
  7.2 214.1 %all-gather.3.cloned.1.call-start = ((), (), s32[]{:S(2)}) async-start(), calls=%async_computation.9 | async-start | bytes 8912896 | tf_op jit(solution)/shard_map/all_gather | solution.py:569
  18.6 343.6 %all-gather.5.cloned.1.call-start = ((), (), s32[]{:S(2)}) async-start(), calls=%async_computation.10 | async-start | bytes 8912896 | tf_op jit(solution)/shard_map/all_gather | solution.py:569
  19.8 41.3 %collective-permute-start.3 = (bf16[128,2048]{1,0:T(8,128)(2,1)}, bf16[128,2048]{1,0:T(8,128)(2,1)}, u32[]{:S(2)}, u32[]{:S(2)}) collective-permute-start(bf16[128,2048]{1,0:T(8,128)(2,1)} %fusion.18.refs_0_), channel_id=1, source_target_pairs={{0,2},{1,3},{4,0},{5,1},{8,4},{9,5},{12,8},{13,9},{14,12},{15,13},... | collective-permute-start | bytes 1572872 | tf_op jit(solution)/shard_map/ppermute | solution.py:261
  21.6 42.0 %collective-permute-start.1 = (bf16[128,2048]{1,0:T(8,128)(2,1)}, bf16[128,2048]{1,0:T(8,128)(2,1)}, u32[]{:S(2)}, u32[]{:S(2)}) collective-permute-start(bf16[128,2048]{1,0:T(8,128)(2,1)} %fusion.18.refs_0_), channel_id=1, source_target_pairs={{0,4},{1,5},{4,8},{5,9},{8,12},{9,13},{12,14},{13,15},{14,10},{15,... | collective-permute-start | bytes 1572872 | tf_op jit(solution)/shard_map/ppermute | solution.py:261
  29.0 113.6 %collective-permute-start.20 = (bf16[256,2816]{1,0:T(8,128)(2,1)}, bf16[256,2816]{1,0:T(8,128)(2,1)}, u32[]{:S(2)}, u32[]{:S(2)}) collective-permute-start(bf16[256,2816]{1,0:T(8,128)(2,1)} %get-tuple-element.80), channel_id=1, source_target_pairs={{0,16},{16,0},{1,17},{17,1},{2,18},{18,2},{3,19},{19,3},{4,20},{20... | collective-permute-start | bytes 4325384 | tf_op jit(solution)/shard_map/ppermute | solution.py:630
  29.3 64.6 %collective-permute-start.15 = (bf16[256,2816]{1,0:T(8,128)(2,1)}, bf16[256,2816]{1,0:T(8,128)(2,1)}, u32[]{:S(2)}, u32[]{:S(2)}) collective-permute-start(bf16[256,2816]{1,0:T(8,128)(2,1)} %get-tuple-element.81), channel_id=1, source_target_pairs={{0,16},{16,0},{1,17},{17,1},{2,18},{18,2},{3,19},{19,3},{4,20},{20... | collective-permute-start | bytes 4325384 | tf_op jit(solution)/shard_map/ppermute | solution.py:630
  34.6 60.6 %all-to-all-start = ((bf16[16,64,384]{2,1,0:T(8,128)(2,1)}), bf16[16,64,384]{2,1,0:T(8,128)(2,1)}, u32[]{:S(2)}, u32[]{:S(2)}) async-start(bf16[16,64,384]{2,1,0:T(8,128)(2,1)} %reshape.457), calls=%async_computation | async-start | bytes 1572864 | tf_op jit(solution)/shard_map/all_to_all | solution.py:573
  61.1 44.3 %collective-permute-start.7 = (bf16[128,2048]{1,0:T(8,128)(2,1)}, bf16[128,2048]{1,0:T(8,128)(2,1)}, u32[]{:S(2)}, u32[]{:S(2)}) collective-permute-start(bf16[128,2048]{1,0:T(8,128)(2,1)} %collective-permute-done.3.refs_4_), channel_id=1, source_target_pairs={{0,2},{1,3},{4,0},{5,1},{8,4},{9,5},{12,8},{13,9},{14,12},{15,13},... | collective-permute-start | bytes 1572872 | tf_op jit(solution)/shard_map/ppermute | solution.py:261
  63.6 78.3 %collective-permute-start.4 = (bf16[128,2048]{1,0:T(8,128)(2,1)}, bf16[128,2048]{1,0:T(8,128)(2,1)}, u32[]{:S(2)}, u32[]{:S(2)}) collective-permute-start(bf16[128,2048]{1,0:T(8,128)(2,1)} %collective-permute-done.3.refs_4_), channel_id=1, source_target_pairs={{0,1},{1,0},{2,3},{3,2},{4,5},{5,4},{6,7},{7,6},{8,9},{9,8},{10,11... | collective-permute-start | bytes 1572872 | tf_op jit(solution)/shard_map/ppermute | solution.py:266
  63.6 44.3 %collective-permute-start.5 = (bf16[128,2048]{1,0:T(8,128)(2,1)}, bf16[128,2048]{1,0:T(8,128)(2,1)}, u32[]{:S(2)}, u32[]{:S(2)}) collective-permute-start(bf16[128,2048]{1,0:T(8,128)(2,1)} %collective-permute-done.1.refs_2_), channel_id=1, source_target_pairs={{0,4},{1,5},{4,8},{5,9},{8,12},{9,13},{12,14},{13,15},{14,10},{15,... | collective-permute-start | bytes 1572872 | tf_op jit(solution)/shard_map/ppermute | solution.py:261
  94.0 48.6 %collective-permute-start.2 = (bf16[128,2048]{1,0:T(8,128)(2,1)}, bf16[128,2048]{1,0:T(8,128)(2,1)}, u32[]{:S(2)}, u32[]{:S(2)}) collective-permute-start(bf16[128,2048]{1,0:T(8,128)(2,1)} %collective-permute-done.1.refs_2_), channel_id=1, source_target_pairs={{0,1},{1,0},{2,3},{3,2},{4,5},{5,4},{6,7},{7,6},{8,9},{9,8},{10,11... | collective-permute-start | bytes 1572872 | tf_op jit(solution)/shard_map/ppermute | solution.py:266
  99.3 95.7 %all-to-all-start.1 = ((bf16[16,64,352]{2,1,0:T(8,128)(2,1)}), bf16[16,64,352]{2,1,0:T(8,128)(2,1)}, u32[]{:S(2)}, u32[]{:S(2)}) async-start(bf16[16,64,352]{2,1,0:T(8,128)(2,1)} %multiply_convert_fusion.9), calls=%async_computation.1 | async-start | bytes 1572864 | tf_op jit(solution)/shard_map/all_to_all | solution.py:573
  163.1 49.8 %collective-permute-start.22 = (bf16[256,2816]{1,0:T(8,128)(2,1)}, bf16[256,2816]{1,0:T(8,128)(2,1)}, u32[]{:S(2)}, u32[]{:S(2)}) collective-permute-start(bf16[256,2816]{1,0:T(8,128)(2,1)} %get-tuple-element.79), channel_id=1, source_target_pairs={{0,16},{16,0},{1,17},{17,1},{2,18},{18,2},{3,19},{19,3},{4,20},{20... | collective-permute-start | bytes 4325384 | tf_op jit(solution)/shard_map/ppermute | solution.py:630
  203.8 411.4 %reduce-scatter.3.cloned.1.call-start = ((), (), s32[]{:S(2)}) async-start(), calls=%async_computation.11 | async-start | bytes 8912896 | tf_op jit(solution)/shard_map/reduce_scatter | solution.py:753
  209.7 67.5 %collective-permute-start.32 = (bf16[256,2816]{1,0:T(8,128)(2,1)}, bf16[256,2816]{1,0:T(8,128)(2,1)}, u32[]{:S(2)}, u32[]{:S(2)}) collective-permute-start(bf16[256,2816]{1,0:T(8,128)(2,1)} %get-tuple-element.78), channel_id=1, source_target_pairs={{0,16},{16,0},{1,17},{17,1},{2,18},{18,2},{3,19},{19,3},{4,20},{20... | collective-permute-start | bytes 4325384 | tf_op jit(solution)/shard_map/ppermute | solution.py:630
  214.8 78.9 %collective-permute-start.43 = (bf16[16,64,352]{2,1,0:T(8,128)(2,1)}, bf16[16,64,352]{2,1,0:T(8,128)(2,1)}, u32[]{:S(2)}, u32[]{:S(2)}) collective-permute-start(bf16[16,64,352]{2,1,0:T(8,128)(2,1)} %all-to-all-done.1), channel_id=1, source_target_pairs={{0,16},{16,0},{1,17},{17,1},{2,18},{18,2},{3,19},{19,3},{4,20},{20... | collective-permute-start | bytes 2162696 | tf_op jit(solution)/shard_map/ppermute | solution.py:223
  228.9 54.2 %collective-permute-start.26 = (bf16[128,2176]{1,0:T(8,128)(2,1)S(1)}, bf16[128,2176]{1,0:T(8,128)(2,1)}, u32[]{:S(2)}, u32[]{:S(2)}) collective-permute-start(bf16[128,2176]{1,0:T(8,128)(2,1)S(1)} %concatenate.56.refs_0_), channel_id=1, source_target_pairs={{0,2},{1,3},{4,0},{5,1},{8,4},{9,5},{12,8},{13,9},{14,12},{15,13},... | collective-permute-start | bytes 1671176 | tf_op jit(solution)/shard_map/ppermute | solution.py:261
  336.3 47.2 %collective-permute-start.42 = (bf16[352,2048]{1,0:T(8,128)(2,1)}, bf16[352,2048]{1,0:T(8,128)(2,1)}, u32[]{:S(2)}, u32[]{:S(2)}) collective-permute-start(bf16[352,2048]{1,0:T(8,128)(2,1)} %get-tuple-element.85), channel_id=1, source_target_pairs={{0,16},{16,0},{1,17},{17,1},{2,18},{18,2},{3,19},{19,3},{4,20},{20... | collective-permute-start | bytes 4325384 | tf_op jit(solution)/shard_map/ppermute | solution.py:630
  511.1 43.4 %collective-permute-start.82 = (bf16[16,64,352]{2,1,0:T(8,128)(2,1)S(1)}, bf16[16,64,352]{2,1,0:T(8,128)(2,1)S(1)}, u32[]{:S(2)}, u32[]{:S(2)}) collective-permute-start(bf16[16,64,352]{2,1,0:T(8,128)(2,1)S(1)} %fusion.32), channel_id=1, source_target_pairs={{0,16},{16,0},{1,17},{17,1},{2,18},{18,2},{3,19},{19,3},{4,20},{20... | collective-permute-start | bytes 2162696 | tf_op jit(solution)/shard_map/ppermute | solution.py:243
  512.2 82.8 %collective-permute-start.45 = (bf16[128,2176]{1,0:T(8,128)(2,1)S(1)}, bf16[128,2176]{1,0:T(8,128)(2,1)S(1)}, u32[]{:S(2)}, u32[]{:S(2)}) collective-permute-start(bf16[128,2176]{1,0:T(8,128)(2,1)S(1)} %copy-done.43), channel_id=1, source_target_pairs={{0,1},{1,0},{2,3},{3,2},{4,5},{5,4},{6,7},{7,6},{8,9},{9,8},{10,11... | collective-permute-start | bytes 1671176 | tf_op jit(solution)/shard_map/ppermute | solution.py:266
  513.2 49.9 %collective-permute-start.55 = (bf16[128,2176]{1,0:T(8,128)(2,1)S(1)}, bf16[128,2176]{1,0:T(8,128)(2,1)S(1)}, u32[]{:S(2)}, u32[]{:S(2)}) collective-permute-start(bf16[128,2176]{1,0:T(8,128)(2,1)S(1)} %copy-done.45), channel_id=1, source_target_pairs={{0,1},{1,0},{2,3},{3,2},{4,5},{5,4},{6,7},{7,6},{8,9},{9,8},{10,11... | collective-permute-start | bytes 1671176 | tf_op jit(solution)/shard_map/ppermute | solution.py:266
  513.7 72.6 %collective-permute-start.54 = (bf16[128,2176]{1,0:T(8,128)(2,1)S(1)}, bf16[128,2176]{1,0:T(8,128)(2,1)S(1)}, u32[]{:S(2)}, u32[]{:S(2)}) collective-permute-start(bf16[128,2176]{1,0:T(8,128)(2,1)S(1)} %copy-done.44), channel_id=1, source_target_pairs={{0,1},{1,0},{2,3},{3,2},{4,5},{5,4},{6,7},{7,6},{8,9},{9,8},{10,11... | collective-permute-start | bytes 1671176 | tf_op jit(solution)/shard_map/ppermute | solution.py:266
  647.5 87.0 %collective-permute-start.71 = (bf16[256,2816]{1,0:T(8,128)(2,1)}, bf16[256,2816]{1,0:T(8,128)(2,1)}, u32[]{:S(2)}, u32[]{:S(2)}) collective-permute-start(bf16[256,2816]{1,0:T(8,128)(2,1)} %convolution_convert_fusion.5), channel_id=1, source_target_pairs={{0,16},{16,0},{1,17},{17,1},{2,18},{18,2},{3,19},{19,3},{4,20},{20... | collective-permute-start | bytes 4325384 | tf_op jit(solution)/shard_map/ppermute | solution.py:761
  649.3 63.5 %collective-permute-start.68 = (bf16[352,2048]{1,0:T(8,128)(2,1)}, bf16[352,2048]{1,0:T(8,128)(2,1)}, u32[]{:S(2)}, u32[]{:S(2)}) collective-permute-start(bf16[352,2048]{1,0:T(8,128)(2,1)} %convolution_convert_fusion.6), channel_id=1, source_target_pairs={{0,16},{16,0},{1,17},{17,1},{2,18},{18,2},{3,19},{19,3},{4,20},{20... | collective-permute-start | bytes 4325384 | tf_op jit(solution)/shard_map/ppermute | solution.py:761
  658.8 65.0 %all-to-all-start.5 = ((bf16[16,64,352]{2,1,0:T(8,128)(2,1)}), bf16[16,64,352]{2,1,0:T(8,128)(2,1)}, u32[]{:S(2)}, u32[]{:S(2)}) async-start(bf16[16,64,352]{2,1,0:T(8,128)(2,1)} %fusion.14), calls=%async_computation.7 | async-start | bytes 1572864 | tf_op jit(solution)/shard_map/all_to_all | solution.py:573
  665.2 225.1 %reduce-scatter.5.cloned.1.call-start = ((), (), s32[]{:S(2)}) async-start(), calls=%async_computation.12 | async-start | bytes 8912896 | tf_op jit(solution)/shard_map/reduce_scatter | solution.py:815
  721.8 164.5 %collective-permute-start.86 = (bf16[256,2816]{1,0:T(8,128)(2,1)}, bf16[256,2816]{1,0:T(8,128)(2,1)}, u32[]{:S(2)}, u32[]{:S(2)}) collective-permute-start(bf16[256,2816]{1,0:T(8,128)(2,1)} %convolution_convert_fusion.2), channel_id=1, source_target_pairs={{0,16},{16,0},{1,17},{17,1},{2,18},{18,2},{3,19},{19,3},{4,20},{20... | collective-permute-start | bytes 4325384 | tf_op jit(solution)/shard_map/ppermute | solution.py:761
  723.5 133.2 %collective-permute-start.84 = (bf16[256,2816]{1,0:T(8,128)(2,1)}, bf16[256,2816]{1,0:T(8,128)(2,1)}, u32[]{:S(2)}, u32[]{:S(2)}) collective-permute-start(bf16[256,2816]{1,0:T(8,128)(2,1)} %convolution_convert_fusion.4), channel_id=1, source_target_pairs={{0,16},{16,0},{1,17},{17,1},{2,18},{18,2},{3,19},{19,3},{4,20},{20... | collective-permute-start | bytes 4325384 | tf_op jit(solution)/shard_map/ppermute | solution.py:761
  754.6 55.3 %all-to-all-start.6 = ((f32[32,1,1088]{2,1,0:T(1,128)}), f32[32,1,1088]{2,1,0:T(1,128)S(1)}, u32[]{:S(2)}, u32[]{:S(2)}) async-start(f32[32,1,1088]{2,1,0:T(1,128)} %reshape.517), calls=%async_computation.8 | async-start | bytes 294912 | tf_op jit(solution)/shard_map/all_to_all | solution.py:821
  760.2 44.9 %collective-permute-start.80 = (bf16[16,64,384]{2,1,0:T(8,128)(2,1)S(1)}, bf16[16,64,384]{2,1,0:T(8,128)(2,1)S(1)}, u32[]{:S(2)}, u32[]{:S(2)}) collective-permute-start(bf16[16,64,384]{2,1,0:T(8,128)(2,1)S(1)} %fusion.31), channel_id=1, source_target_pairs={{0,16},{16,0},{1,17},{17,1},{2,18},{18,2},{3,19},{19,3},{4,20},{20... | collective-permute-start | bytes 2359304 | tf_op jit(solution)/shard_map/ppermute | solution.py:243
  762.0 44.1 %collective-permute-start.74 = (bf16[128,2048]{1,0:T(8,128)(2,1)S(1)}, bf16[128,2048]{1,0:T(8,128)(2,1)S(1)}, u32[]{:S(2)}, u32[]{:S(2)}) collective-permute-start(bf16[128,2048]{1,0:T(8,128)(2,1)S(1)} %copy-done.54), channel_id=1, source_target_pairs={{0,1},{1,0},{2,3},{3,2},{4,5},{5,4},{6,7},{7,6},{8,9},{9,8},{10,11... | collective-permute-start | bytes 1572872 | tf_op jit(solution)/shard_map/ppermute | solution.py:266
  805.1 43.9 %collective-permute-start.62 = (bf16[128,2048]{1,0:T(8,128)(2,1)S(1)}, bf16[128,2048]{1,0:T(8,128)(2,1)}, u32[]{:S(2)}, u32[]{:S(2)}) collective-permute-start(bf16[128,2048]{1,0:T(8,128)(2,1)S(1)} %copy-done.53), channel_id=1, source_target_pairs={{0,1},{1,0},{2,3},{3,2},{4,5},{5,4},{6,7},{7,6},{8,9},{9,8},{10,11... | collective-permute-start | bytes 1572872 | tf_op jit(solution)/shard_map/ppermute | solution.py:266
  (147 other events, 2225.0 us)
Sparse Core Ops, SparseCore 0:
  18.7 101.0 all-gather.2
  122.0 87.2 all-gather.4
  483.6 127.0 reduce-scatter.2
  696.0 126.7 reduce-scatter.4
where the time goes:
time: 919 us; the launch traced here: 907 us
  waiting for transfers between devices  293 us (32%)
  Pallas kernels  148 us (16%)
  starting transfers between devices  144 us (16%)
  matrix products  110 us (12%)
  other arithmetic  90.7 us (10%)
  local copies, waits for them, and re-layouts  89.9 us (10%)
  between operations  31.6 us (3%)
    ppermute x32, waiting for transfers between devices, ring_shift(): return lax.ppermute(value, 'expert', perm)  128 us
    ppermute x6, waiting for transfers between devices, spread(): lax.ppermute(shard[j * size:(j + 1) * size], 'dp', [(i, (i - step) % n_dp...  75.3 us
    dot_general x12, matrix products, dot_tn(): lax.dot_general(left, right, (((0,), (0,)), ((), ())), preferred_element_...  73.7 us
    ppermute x32, starting transfers between devices, ring_shift(): return lax.ppermute(value, 'expert', perm)  59.5 us
    pallas_call x1, Pallas kernels, expert(): pl.pallas_call(functools.partial(expert_kernel, len(ups)), out_shape=[jax...  54.7 us
    all_to_all x6, starting transfers between devices, swap(): lax.all_to_all(value, 'expert', split_axis=0, concat_axis=0, tiled=True)  39.7 us
    ppermute x5, waiting for transfers between devices, dp_gather(): lax.ppermute(value, 'dp', [(i, (i - step) % count) for i in range(count)])  31.5 us
    pallas_call x1, Pallas kernels, attend(): pl.pallas_call(functools.partial(attend_kernel, sources, block), out_shap...  29.2 us
  transfers between devices with their start and end apart: 98, of which 33 were waited for; matrix products, arithmetic and copies ran while one was open for 27% of the time, Pallas kernels for 9%

commit v1 on v0

--- a/solution.py
+++ b/solution.py
@@ -654,9 +654,8 @@
     norm_blocks = ring_gather(
         normed_one.astype(BF16),
         {
-            half - 1: lambda blocks: [head_sent(blocks)],
-            half: lambda blocks: [head_whole(blocks), cos_table, sin_table, extra, share_w]
-            + up_tokens[0],
+            half - 1: lambda blocks: [head_sent(blocks)] + up_tokens[0],
+            half: lambda blocks: [head_whole(blocks), cos_table, sin_table, extra, share_w],
         },
     )
     head_sent_w, head_w = head_w
@@ -665,11 +664,11 @@
         norm_blocks, order, head_w, cos_table, sin_table, first_place
     )
     mixed = jnp.concatenate([head_out.reshape(n_e, count, HEAD_DIM), extra], axis=1)
-    share_w = swap(tied(share_w, head_sent_w))
-    mixed = swap(tied(mixed, share_w, *up_tokens[1]))
+    mixed = swap(tied(mixed, *up_tokens[1]) if up_tokens[1] else mixed)
     small = mixed[:, count:]
     mixed = mixed[:, :count].transpose(1, 0, 2).reshape(count, n_dp, n_e, rows)
     mixed = mixed.transpose(0, 2, 1, 3).reshape(count, width)
+    share_w = swap(tied(share_w, lse))
     proj_all = gather_all(dp_gather(attn_out).reshape(n_dp * rows, width))
     routes_all = small[:, n_e + 1 : n_e + 1 + TOP].astype(F32)
     small = small[:, : n_e + 1].reshape(n_e, n_e + 1, n_dp, rows).transpose(1, 2, 0, 3)
@@ -700,8 +699,8 @@
     norm_blocks = ring_gather(
         payload,
         {
-            half - 1: lambda blocks: [share_sent] + up_tokens[3],
-            half: lambda blocks: first(down_parts[1]) + [share_sent],
+            half - 2: lambda blocks: [share_sent] + up_tokens[3],
+            half: lambda blocks: first(down_parts[1]),
         },
     )
 
@@ -741,9 +740,8 @@
     norm_two_part = combine(
         packing, order, steady, me, row_grad, gate_grad, shared_pre_grad, share_w, True, 128
     )
-    marks = []
     norm_two_grad = ring_scatter(
-        lambda n: norm_two_part[n * count : (n + 1) * count], None, marks
+        lambda n: norm_two_part[n * count : (n + 1) * count]
     )
     gate_grad = norm_two_grad[:, width : width + n_e] + norm_two_grad[:, width + 64 : width + 64 + n_e]
     norm_two_grad = norm_two_grad[:, :width]
@@ -755,7 +753,7 @@
     def shard_grads(left, right, chunks):
         size = left.shape[1] // n_dp
         part = size // chunks
-        cut = lambda start, wide: tied(lax.dynamic_slice_in_dim(left, start, wide, 1), *marks)
+        cut = lambda start, wide: lax.dynamic_slice_in_dim(left, start, wide, 1)
         got = [
             [
                 lax.ppermute(
@@ -799,16 +797,17 @@
         logit_grad, router_full.astype(F32), precision=HIGHEST, preferred_element_type=F32
     )
     gain_two_grad = jnp.sum(norm_two_grad * normed_two, axis=0)
-    upstream = cotangent.astype(F32)
+    upstream = tied(cotangent.astype(F32), *down_got[0])
     scaled_two = norm_two_grad * gain_second
     resid_grad = upstream + inverse_two * (
         scaled_two - normed_two * jnp.mean(scaled_two * normed_two, axis=-1, keepdims=True)
     )
     small_grad = jnp.concatenate([router_grad, gain_two_grad[None]], axis=0)
+    small_grad = jnp.pad(small_grad, ((0, HEAD_DIM - n_e - 1), (0, 0))).T
 
     branch_cot = resid_grad.astype(BF16)
     proj_grad = dot_tn(mixed, branch_cot).astype(BF16)
-    mixed_grad = tied(dot_nt(branch_cot, proj_all), proj_grad, *down_got[0]).astype(BF16)
+    mixed_grad = tied(dot_nt(branch_cot, proj_all), *down_got[1]).astype(BF16)
     mixed_grad = mixed_grad.reshape(count, n_e, n_dp, rows).transpose(0, 2, 1, 3)
     mixed_grad = swap(mixed_grad.reshape(count, n_e, HEAD_DIM).transpose(1, 0, 2))
     mixed_grad = mixed_grad.reshape(length, HEAD_DIM)
@@ -817,25 +816,26 @@
     qkv_grad = attend_back(
         query, key, value, mixed_grad, lse, first_place, cos_table, sin_table, order
     )
-    small_grad = tied(small_grad, qkv_grad).reshape(n_e + 1, n_dp * n_e, rows).transpose(1, 0, 2)
-    small_grad = lax.all_to_all(
-        small_grad, ("dp", "expert"), split_axis=0, concat_axis=0, tiled=True
-    )
-    small_grad = jnp.sum(small_grad, axis=0)
     norm_one_part = dot_nt(qkv_grad, head_w).astype(BF16)
     scaled_one = ring_scatter(
         lambda n: norm_one_part[n * count : (n + 1) * count],
-        {1: down_got[1], half - 1: up_got[0]},
-    )
-    expert_out_grad = shard_sum(down_own, down_got, [mixed_grad, scaled_one])
+        {1: up_got[0], half - 1: up_got[min(1, len(up_got) - 1)]},
+    )
+    expert_out_grad = shard_sum(down_own, down_got, [norm_two_grad, mixed_grad])
     expert_in_grad = shard_sum(up_own, up_got, ([qkv_grad] + [scaled_one] * 3)[: len(up_got)])
     input_grad = resid_grad + inverse_one * (
         scaled_one - normed_one * jnp.mean(scaled_one * normed_one, axis=-1, keepdims=True)
     )
-    head_grad = dot_tn(norm_all, qkv_grad).reshape(n_dp, n_e, rows, 3 * HEAD_DIM)
-    head_grad = swap(dp_scatter(head_grad).astype(BF16)).astype(F32)
+    wide = 3 * HEAD_DIM
+    head_grad = jnp.concatenate([dot_tn(norm_all, qkv_grad), small_grad], axis=1)
+    head_grad = dp_scatter(head_grad.reshape(n_dp, n_e, rows, wide + small_grad.shape[1]))
+    head_grad = swap(head_grad.astype(BF16)).astype(F32)
+    small_grad = jnp.sum(head_grad[:, :, wide:], axis=0)
     head_grad = (
-        head_grad.reshape(n_e, rows, 3, HEAD_DIM).transpose(1, 2, 0, 3).reshape(rows, 3 * width)
+        head_grad[:, :, :wide]
+        .reshape(n_e, rows, 3, HEAD_DIM)
+        .transpose(1, 2, 0, 3)
+        .reshape(rows, 3 * width)
     )
     gain_attn_grad = jnp.sum(head_grad * attn_in.astype(F32), axis=1)
     attn_in_grad = head_grad * gain_rows
@@ -847,8 +847,8 @@
         gain_attn_grad,
         share_in_grad,
         share_out_grad,
-        small_grad[:n_e].T,
-        small_grad[n_e],
+        small_grad[:, :n_e],
+        small_grad[:, n_e],
         expert_in_grad,
         expert_out_grad,
     )

time: 919 us -> 916 us (level)
  waiting for transfers between devices: 293 us -> 312 us
  starting transfers between devices: 144 us -> 126 us
    ppermute x32, waiting for transfers between devices: 128 us -> 204 us  [ring_shift(): return lax.ppermute(value, 'expert', perm)]
    ppermute x6, waiting for transfers between devices: 75.3 us -> 58.6 us  [spread(): lax.ppermute(shard[j * size:(j + 1) * size], 'dp', [(i, (i - step) % n_dp...]
    ppermute x5, waiting for transfers between devices: 31.5 us -> 19.5 us  [dp_gather(): lax.ppermute(value, 'dp', [(i, (i - step) % count) for i in range(count)])]
    ppermute x6, waiting for transfers between devices: 25 us -> 14.6 us  [shard_grads(): lax.ppermute(dot_tn(cut((here + step) % n_dp * size + j * part, part), ri...]
    all_to_all x6, waiting for transfers between devices: 16.5 us -> 6.45 us  [swap(): lax.all_to_all(value, 'expert', split_axis=0, concat_axis=0, tiled=True)]
  transfers between devices with their start and end apart: 98 -> 97, of which waited for: 33 -> 31; matrix products, arithmetic and copies ran while one was open for 27% -> 30% of each run, Pallas kernels for 9% -> 9%
where the time goes in v1:
time: 916 us; the launch traced here: 901 us
  waiting for transfers between devices  312 us (34%)
  Pallas kernels  140 us (15%)
  starting transfers between devices  126 us (14%)
  matrix products  107 us (12%)
  local copies, waits for them, and re-layouts  98.1 us (11%)
  other arithmetic  88.8 us (10%)
  between operations  30.3 us (3%)
    ppermute x32, waiting for transfers between devices, ring_shift(): return lax.ppermute(value, 'expert', perm)  204 us
    dot_general x12, matrix products, dot_tn(): lax.dot_general(left, right, (((0,), (0,)), ((), ())), preferred_element_...  71.2 us
    ppermute x6, waiting for transfers between devices, spread(): lax.ppermute(shard[j * size:(j + 1) * size], 'dp', [(i, (i - step) % n_dp...  58.6 us
    ppermute x32, starting transfers between devices, ring_shift(): return lax.ppermute(value, 'expert', perm)  51.3 us
    pallas_call x1, Pallas kernels, expert(): pl.pallas_call(functools.partial(expert_kernel, len(ups)), out_shape=[jax...  46.1 us
    all_to_all x6, starting transfers between devices, swap(): lax.all_to_all(value, 'expert', split_axis=0, concat_axis=0, tiled=True)  33.4 us
    pallas_call x1, Pallas kernels, attend(): pl.pallas_call(functools.partial(attend_kernel, sources, block), out_shap...  29.2 us
    pallas_call x2, Pallas kernels, dispatch(): pl.pallas_call(functools.partial(dispatch_kernel, sources, tuple(widths),...  28.8 us
  transfers between devices with their start and end apart: 97, of which 31 were waited for; matrix products, arithmetic and copies ran while one was open for 30% of the time, Pallas kernels for 9%

profile of v1, /device:TPU:0, one launch (start us, length us, event | category | flops | bytes accessed | tf_op | source)
XLA Modules:
  0.0 901.2 jit_solution(6171003691545262106)
XLA Ops:
  67.8 26.9 %collective-permute-done.9.refs_1_ = bf16[256,2816]{1,0:T(8,128)(2,1)} collective-permute-done((bf16[256,2816]{1,0:T(8,128)(2,1)}, bf16[256,2816]{1,0:T(8,128)(2,1)}, u32[]{:S(2)}, u32[]{:S(2)}) %collective-permute-start.9) | collective-permute-done | bytes 1441824 | tf_op jit(solution)/shard_map/ppermute | solution.py:630
  105.6 13.0 %collective-permute-done.14 = bf16[16,64,384]{2,1,0:T(8,128)(2,1)S(1)} collective-permute-done((bf16[16,64,384]{2,1,0:T(8,128)(2,1)}, bf16[16,64,384]{2,1,0:T(8,128)(2,1)S(1)}, u32[]{:S(2)}, u32[]{:S(2)}) %collective-permute-start.14) | collective-permute-done | bytes 786464 | tf_op jit(solution)/shard_map/ppermute | solution.py:223
  146.5 9.7 %collective-permute-done.17.refs_15_ = bf16[64,2048]{1,0:T(8,128)(2,1)S(1)} collective-permute-done((bf16[64,2048]{1,0:T(8,128)(2,1)S(1)}, bf16[64,2048]{1,0:T(8,128)(2,1)S(1)}, u32[]{:S(2)}, u32[]{:S(2)}) %collective-permute-start.17) | collective-permute-done | bytes 262176 | tf_op jit(solution)/shard_map/ppermute | solution.py:261
  159.9 29.2 %attend.1 = (bf16[2048,128]{1,0:T(8,128)(2,1)S(1)}, bf16[2048,128]{1,0:T(8,128)(2,1)}, bf16[2048,128]{1,0:T(8,128)(2,1)}, bf16[2048,128]{1,0:T(8,128)(2,1)}, f32...) custom-call(s32[16]{0:T(128)S(1)} %fusion.61.order_ref.to_ref, bf16[128,2048]{1,0:T(8,128)(2,1)} %fusion.16.refs_0_, ...), custom_call_target="tpu_custom_call" | custom-call | tf_op jit(solution)/shard_map/attend/pallas_call | solution.py:123
  231.9 31.7 %collective-permute-done.28.refs_4_ = bf16[256,2816]{1,0:T(8,128)(2,1)} collective-permute-done((bf16[256,2816]{1,0:T(8,128)(2,1)}, bf16[256,2816]{1,0:T(8,128)(2,1)}, u32[]{:S(2)}, u32[]{:S(2)}) %collective-permute-start.28) | collective-permute-done | bytes 1441824 | tf_op jit(solution)/shard_map/ppermute | solution.py:630
  270.0 10.9 %collective-permute-done.24.refs_2_ = bf16[128,2176]{1,0:T(8,128)(2,1)S(1)} collective-permute-done((bf16[128,2176]{1,0:T(8,128)(2,1)S(1)}, bf16[128,2176]{1,0:T(8,128)(2,1)S(1)}, u32[]{:S(2)}, u32[]{:S(2)}) %collective-permute-start.24) | collective-permute-done | bytes 557088 | tf_op jit(solution)/shard_map/ppermute | solution.py:261
  289.0 6.6 collective-permute-done.29.refs_6_
  298.7 12.2 %collective-permute-done.33.refs_10_ = bf16[128,2176]{1,0:T(8,128)(2,1)S(1)} collective-permute-done((bf16[128,2176]{1,0:T(8,128)(2,1)}, bf16[128,2176]{1,0:T(8,128)(2,1)S(1)}, u32[]{:S(2)}, u32[]{:S(2)}) %collective-permute-start.33) | collective-permute-done | bytes 557088 | tf_op jit(solution)/shard_map/ppermute | solution.py:261
  323.5 14.2 %dispatch.2 = (bf16[2048,2048]{1,0:T(8,128)(2,1)}, bf16[2048,128]{1,0:T(8,128)(2,1)S(1)}, bf16[1280,2048]{1,0:T(8,128)(2,1)}, f32[1280,1]{1,0:T(8,128)}) custom-call(s32[16]{0:T(128)S(1)} %fusion.60.base_ref, s32[16]{0:T(128)S(1)} %fusion.61.order_ref.to_ref, s32[16,1,128]{2,1,0:T(1,128)S(1)} %fusion.46.pos_ref, ...), custom_call_target="tpu_custom_call" | custom-call | tf_op jit(solution)/shard_map/dispatch/pallas_call | solution.py:415
  337.6 8.6 fusion.70
  346.5 14.6 %dispatch.3 = (bf16[1280,2048]{1,0:T(8,128)(2,1)}, f32[1280,1]{1,0:T(8,128)S(1)}) custom-call(s32[16]{0:T(128)S(1)} %fusion.60.base_ref, s32[16]{0:T(128)S(1)} %fusion.61.order_ref.to_ref, s32[16,1,128]{2,1,0:T(1,128)S(1)} %fusion.46.pos_ref, f32[16,1,128]{2,1,0:T(1,128)S(1)} %bitcast.220, bf16[2048,2048]{1,0:T(8,128)(2,1)} %all-gather.5.cloned.1.call-done.refs_0_), custom_call_target="tpu_custom_call" | custom-call | tf_op jit(solution)/shard_map/dispatch/pallas_call | solution.py:415
  361.1 8.4 multiply_convert_fusion.1
  369.5 46.1 %expert.1 = (bf16[1280,2048]{1,0:T(8,128)(2,1)}, bf16[1280,2048]{1,0:T(8,128)(2,1)}, bf16[1280,1408]{1,0:T(8,128)(2,1)}, bf16[1280,2048]{1,0:T(8,128)(2,1)}, bf1...) custom-call(s32[1]{0:T(128)} %bitcast.37.total_ref, s32[8]{0:T(128)} %stack.89.starts_ref, ...), custom_call_target="tpu_custom_call" | custom-call | tf_op jit(solution)/shard_map/expert/pallas_call | solution.py:498
  418.1 11.0 %combine.2 = bf16[2048,2048]{1,0:T(8,128)(2,1)} custom-call(s32[16]{0:T(128)S(1)} %fusion.60.base_ref, s32[16]{0:T(128)S(1)} %fusion.61.order_ref.to_ref, s32[16]{0:T(128)S(1)} %fusion.61.order_ref.to_ref, s32[1]{0:T(128)} %bitcast.34.me_ref, s32[16,1,128]{2,1,0:T(1,128)S(1)} %fusion.46.pos_ref, bf16[1280,2048]{1,0:T(8,128)(2,1)S(1)} %copy-done.3, ...), custom_call_target="tpu_custom_call" | custom-call | tf_op jit(solution)/shard_map/combine/pallas_call | solution.py:546
  433.9 14.0 %combine.3 = bf16[2048,2176]{1,0:T(8,128)(2,1)} custom-call(s32[16]{0:T(128)S(1)} %fusion.60.base_ref, s32[16]{0:T(128)S(1)} %fusion.61.order_ref.to_ref, s32[16]{0:T(128)S(1)} %iota.41.to_ref, s32[1]{0:T(128)} %bitcast.34.me_ref, s32[16,1,128]{2,1,0:T(1,128)S(1)} %fusion.46.pos_ref, bf16[1280,2048]{1,0:T(8,128)(2,1)S(1)} %copy-done.2, ...), custom_call_target="tpu_custom_call" | custom-call | tf_op jit(solution)/shard_map/combine/pallas_call | solution.py:546
  451.9 9.1 %collective-permute-start.50 = (bf16[128,2176]{1,0:T(8,128)(2,1)S(1)}, bf16[128,2176]{1,0:T(8,128)(2,1)S(1)}, u32[]{:S(2)}, u32[]{:S(2)}) collective-permute-start(bf16[128,2176]{1,0:T(8,128)(2,1)S(1)} %get-tuple-element.103), channel_id=1, source_target_pairs={{0,1},{1,0},{2,3},{3,2},{4,5},{5,4},{6,7},{7,6},{8,9},{9,8},{10,11... | collective-permute-start | bytes 1671176 | tf_op jit(solution)/shard_map/ppermute | solution.py:266
  468.3 6.7 convolution_convert_fusion.6
  477.8 10.9 %convolution_bitcast_fusion = f32[1,1024,2816]{2,1,0:T(8,128)} fusion(bf16[1280,2816]{1,0:T(8,128)(2,1)S(1)} %bitcast.222, bf16[1280,2048]{1,0:T(8,128)(2,1)S(1)} %bitcast.233, s32[]{:T(128)S(6)} %select_n.235), kind=kOutput, calls=%fused_computation.3 | convolution fusion | flops 7381975040 | bytes 21364740 | tf_op jit(solution)/shard_map/dot_general | solution.py:54
  488.8 7.6 collective-permute-done.51
  499.1 7.2 fusion.72
  506.5 25.9 %collective-permute-done.52 = bf16[128,2176]{1,0:T(8,128)(2,1)S(1)} collective-permute-done((bf16[128,2176]{1,0:T(8,128)(2,1)}, bf16[128,2176]{1,0:T(8,128)(2,1)S(1)}, u32[]{:S(2)}, u32[]{:S(2)}) %collective-permute-start.52) | collective-permute-done | bytes 557088 | tf_op jit(solution)/shard_map/ppermute | solution.py:261
  537.1 9.7 %collective-permute-done.53 = bf16[128,2176]{1,0:T(8,128)(2,1)S(1)} collective-permute-done((bf16[128,2176]{1,0:T(8,128)(2,1)S(1)}, bf16[128,2176]{1,0:T(8,128)(2,1)S(1)}, u32[]{:S(2)}, u32[]{:S(2)}) %collective-permute-start.53) | collective-permute-done | bytes 557088 | tf_op jit(solution)/shard_map/ppermute | solution.py:261
  550.2 16.7 %collective-permute-done.58 = bf16[64,2176]{1,0:T(8,128)(2,1)S(1)} collective-permute-done((bf16[64,2176]{1,0:T(8,128)(2,1)S(1)}, bf16[64,2176]{1,0:T(8,128)(2,1)S(1)}, u32[]{:S(2)}, u32[]{:S(2)}) %collective-permute-start.58) | collective-permute-done | bytes 278560 | tf_op jit(solution)/shard_map/ppermute | solution.py:261
  567.0 9.3 %convolution_bitcast_fusion.1 = f32[1,704,2048]{2,1,0:T(8,128)} fusion(bf16[1280,2048]{1,0:T(8,128)(2,1)} %get-tuple-element.37, bf16[1280,1408]{1,0:T(8,128)(2,1)S(1)} %copy-done.73, s32[]{:T(128)S(6)} %select_n.238), kind=kOutput, calls=%fused_computation.9 | convolution fusion | flops 3690987520 | bytes 12976132 | tf_op jit(solution)/shard_map/dot_general | solution.py:54
  588.0 6.7 collective-permute-done.60
  627.2 6.6 convolution_convert_fusion.5
  652.2 10.8 %attend_back.1 = bf16[2048,384]{1,0:T(8,128)(2,1)S(1)} custom-call(s32[16]{0:T(128)S(1)} %fusion.61.order_ref.to_ref, bf16[2048,128]{1,0:T(8,128)(2,1)S(1)} %copy-done.9, bf16[2048,128]{1,0:T(8,128)(2,1)S(1)} %copy-done.10, bf16[2048,128]{1,0:T(8,128)(2,1)S(1)} %copy-done.11, bf16[2048,128]{1,0:T(8,128)(2,1)S(1)} %bitcast.215, ...), custom_call_target="tpu_custom_call" | custom-call | tf_op jit(solution)/shard_map/attend_back/pallas_call | solution.py:201
  684.7 14.6 %collective-permute-done.72 = bf16[256,2816]{1,0:T(8,128)(2,1)} collective-permute-done((bf16[256,2816]{1,0:T(8,128)(2,1)}, bf16[256,2816]{1,0:T(8,128)(2,1)}, u32[]{:S(2)}, u32[]{:S(2)}) %collective-permute-start.72) | collective-permute-done | bytes 1441824 | tf_op jit(solution)/shard_map/ppermute | solution.py:759
  721.3 9.0 collective-permute-done.68
  790.4 31.4 %collective-permute-done.77 = bf16[64,2048]{1,0:T(8,128)(2,1)S(1)} collective-permute-done((bf16[64,2048]{1,0:T(8,128)(2,1)S(1)}, bf16[64,2048]{1,0:T(8,128)(2,1)S(1)}, u32[]{:S(2)}, u32[]{:S(2)}) %collective-permute-start.77) | collective-permute-done | bytes 262176 | tf_op jit(solution)/shard_map/ppermute | solution.py:261
  827.7 13.5 %collective-permute-done.78 = bf16[128,2048]{1,0:T(8,128)(2,1)S(1)} collective-permute-done((bf16[128,2048]{1,0:T(8,128)(2,1)S(1)}, bf16[128,2048]{1,0:T(8,128)(2,1)S(1)}, u32[]{:S(2)}, u32[]{:S(2)}) %collective-permute-start.78) | collective-permute-done | bytes 524320 | tf_op jit(solution)/shard_map/ppermute | solution.py:261
  845.5 10.4 %collective-permute-done.79 = bf16[128,2048]{1,0:T(8,128)(2,1)S(1)} collective-permute-done((bf16[128,2048]{1,0:T(8,128)(2,1)S(1)}, bf16[128,2048]{1,0:T(8,128)(2,1)S(1)}, u32[]{:S(2)}, u32[]{:S(2)}) %collective-permute-start.79) | collective-permute-done | bytes 524320 | tf_op jit(solution)/shard_map/ppermute | solution.py:261
  (552 shorter events, 407.7 us)
Async XLA Ops:
  7.2 213.1 %all-gather.3.cloned.1.call-start = ((), (), s32[]{:S(2)}) async-start(), calls=%async_computation.8 | async-start | bytes 8912896 | tf_op jit(solution)/shard_map/all_gather | solution.py:569
  18.7 327.8 %all-gather.5.cloned.1.call-start = ((), (), s32[]{:S(2)}) async-start(), calls=%async_computation.9 | async-start | bytes 8912896 | tf_op jit(solution)/shard_map/all_gather | solution.py:569
  20.6 42.2 %collective-permute-start.3 = (bf16[128,2048]{1,0:T(8,128)(2,1)}, bf16[128,2048]{1,0:T(8,128)(2,1)}, u32[]{:S(2)}, u32[]{:S(2)}) collective-permute-start(bf16[128,2048]{1,0:T(8,128)(2,1)} %fusion.16.refs_0_), channel_id=1, source_target_pairs={{0,2},{1,3},{4,0},{5,1},{8,4},{9,5},{12,8},{13,9},{14,12},{15,13},... | collective-permute-start | bytes 1572872 | tf_op jit(solution)/shard_map/ppermute | solution.py:261
  29.7 104.4 %collective-permute-start.20 = (bf16[256,2816]{1,0:T(8,128)(2,1)}, bf16[256,2816]{1,0:T(8,128)(2,1)}, u32[]{:S(2)}, u32[]{:S(2)}) collective-permute-start(bf16[256,2816]{1,0:T(8,128)(2,1)} %get-tuple-element.125), channel_id=1, source_target_pairs={{0,16},{16,0},{1,17},{17,1},{2,18},{18,2},{3,19},{19,3},{4,20},{20... | collective-permute-start | bytes 4325384 | tf_op jit(solution)/shard_map/ppermute | solution.py:630
  30.0 64.6 %collective-permute-start.9 = (bf16[256,2816]{1,0:T(8,128)(2,1)}, bf16[256,2816]{1,0:T(8,128)(2,1)}, u32[]{:S(2)}, u32[]{:S(2)}) collective-permute-start(bf16[256,2816]{1,0:T(8,128)(2,1)} %get-tuple-element.126), channel_id=1, source_target_pairs={{0,16},{16,0},{1,17},{17,1},{2,18},{18,2},{3,19},{19,3},{4,20},{20... | collective-permute-start | bytes 4325384 | tf_op jit(solution)/shard_map/ppermute | solution.py:630
  35.3 60.5 %all-to-all-start = ((bf16[16,64,384]{2,1,0:T(8,128)(2,1)}), bf16[16,64,384]{2,1,0:T(8,128)(2,1)}, u32[]{:S(2)}, u32[]{:S(2)}) async-start(bf16[16,64,384]{2,1,0:T(8,128)(2,1)} %reshape.436), calls=%async_computation | async-start | bytes 1572864 | tf_op jit(solution)/shard_map/all_to_all | solution.py:573
  42.3 56.1 %collective-permute-start.5 = (bf16[128,2048]{1,0:T(8,128)(2,1)}, bf16[128,2048]{1,0:T(8,128)(2,1)}, u32[]{:S(2)}, u32[]{:S(2)}) collective-permute-start(bf16[128,2048]{1,0:T(8,128)(2,1)} %collective-permute-done.1.refs_2_), channel_id=1, source_target_pairs={{0,4},{1,5},{4,8},{5,9},{8,12},{9,13},{12,14},{13,15},{14,10},{15,... | collective-permute-start | bytes 1572872 | tf_op jit(solution)/shard_map/ppermute | solution.py:261
  67.8 65.7 %collective-permute-start.4 = (bf16[128,2048]{1,0:T(8,128)(2,1)}, bf16[128,2048]{1,0:T(8,128)(2,1)}, u32[]{:S(2)}, u32[]{:S(2)}) collective-permute-start(bf16[128,2048]{1,0:T(8,128)(2,1)} %collective-permute-done.3.refs_4_), channel_id=1, source_target_pairs={{0,1},{1,0},{2,3},{3,2},{4,5},{5,4},{6,7},{7,6},{8,9},{9,8},{10,11... | collective-permute-start | bytes 1572872 | tf_op jit(solution)/shard_map/ppermute | solution.py:266
  141.3 61.3 %collective-permute-start.22 = (bf16[256,2816]{1,0:T(8,128)(2,1)}, bf16[256,2816]{1,0:T(8,128)(2,1)}, u32[]{:S(2)}, u32[]{:S(2)}) collective-permute-start(bf16[256,2816]{1,0:T(8,128)(2,1)} %get-tuple-element.124), channel_id=1, source_target_pairs={{0,16},{16,0},{1,17},{17,1},{2,18},{18,2},{3,19},{19,3},{4,20},{20... | collective-permute-start | bytes 4325384 | tf_op jit(solution)/shard_map/ppermute | solution.py:630
  158.9 71.1 %collective-permute-start.44 = (bf16[88,2048]{1,0:T(8,128)(2,1)}, bf16[88,2048]{1,0:T(8,128)(2,1)}, u32[]{:S(2)}, u32[]{:S(2)}) collective-permute-start(bf16[88,2048]{1,0:T(8,128)(2,1)} %param.22), channel_id=1, source_target_pairs={{0,16},{16,0},{1,17},{17,1},{2,18},{18,2},{3,19},{19,3},{4,20},{20... | collective-permute-start | bytes 1081352 | tf_op jit(solution)/shard_map/ppermute | solution.py:223
  198.5 85.5 %collective-permute-start.37 = (bf16[352,2048]{1,0:T(8,128)(2,1)}, bf16[352,2048]{1,0:T(8,128)(2,1)}, u32[]{:S(2)}, u32[]{:S(2)}) collective-permute-start(bf16[352,2048]{1,0:T(8,128)(2,1)} %get-tuple-element.131), channel_id=1, source_target_pairs={{0,16},{16,0},{1,17},{17,1},{2,18},{18,2},{3,19},{19,3},{4,20},{20... | collective-permute-start | bytes 4325384 | tf_op jit(solution)/shard_map/ppermute | solution.py:630
  199.7 63.9 %collective-permute-start.28 = (bf16[256,2816]{1,0:T(8,128)(2,1)}, bf16[256,2816]{1,0:T(8,128)(2,1)}, u32[]{:S(2)}, u32[]{:S(2)}) collective-permute-start(bf16[256,2816]{1,0:T(8,128)(2,1)} %get-tuple-element.123), channel_id=1, source_target_pairs={{0,16},{16,0},{1,17},{17,1},{2,18},{18,2},{3,19},{19,3},{4,20},{20... | collective-permute-start | bytes 4325384 | tf_op jit(solution)/shard_map/ppermute | solution.py:630
  213.1 51.8 %all-to-all-start.2 = ((bf16[16,64,352]{2,1,0:T(8,128)(2,1)}), bf16[16,64,352]{2,1,0:T(8,128)(2,1)S(1)}, u32[]{:S(2)}, u32[]{:S(2)}) async-start(bf16[16,64,352]{2,1,0:T(8,128)(2,1)} %multiply_convert_fusion.3), calls=%async_computation.2 | async-start | bytes 1572864 | tf_op jit(solution)/shard_map/all_to_all | solution.py:573
  219.1 392.5 %reduce-scatter.3.cloned.1.call-start = ((), (), s32[]{:S(2)}) async-start(), calls=%async_computation.10 | async-start | bytes 8912896 | tf_op jit(solution)/shard_map/reduce_scatter | solution.py:751
  227.3 41.1 %collective-permute-start.26 = (bf16[128,2176]{1,0:T(8,128)(2,1)S(1)}, bf16[128,2176]{1,0:T(8,128)(2,1)}, u32[]{:S(2)}, u32[]{:S(2)}) collective-permute-start(bf16[128,2176]{1,0:T(8,128)(2,1)S(1)} %concatenate.54.refs_0_), channel_id=1, source_target_pairs={{0,2},{1,3},{4,0},{5,1},{8,4},{9,5},{12,8},{13,9},{14,12},{15,13},... | collective-permute-start | bytes 1671176 | tf_op jit(solution)/shard_map/ppermute | solution.py:261
  321.3 48.2 %collective-permute-start.42 = (bf16[352,2048]{1,0:T(8,128)(2,1)}, bf16[352,2048]{1,0:T(8,128)(2,1)}, u32[]{:S(2)}, u32[]{:S(2)}) collective-permute-start(bf16[352,2048]{1,0:T(8,128)(2,1)} %get-tuple-element.130), channel_id=1, source_target_pairs={{0,16},{16,0},{1,17},{17,1},{2,18},{18,2},{3,19},{19,3},{4,20},{20... | collective-permute-start | bytes 4325384 | tf_op jit(solution)/shard_map/ppermute | solution.py:630
  467.4 131.8 %collective-permute-start.45 = (bf16[352,2048]{1,0:T(8,128)(2,1)}, bf16[352,2048]{1,0:T(8,128)(2,1)S(1)}, u32[]{:S(2)}, u32[]{:S(2)}) collective-permute-start(bf16[352,2048]{1,0:T(8,128)(2,1)} %convolution_convert_fusion.7), channel_id=1, source_target_pairs={{0,16},{16,0},{1,17},{17,1},{2,18},{18,2},{3,19},{19,3},{4,20},{20... | collective-permute-start | bytes 4325384 | tf_op jit(solution)/shard_map/ppermute | solution.py:759
  475.0 127.1 %collective-permute-start.62 = (bf16[352,2048]{1,0:T(8,128)(2,1)}, bf16[352,2048]{1,0:T(8,128)(2,1)S(1)}, u32[]{:S(2)}, u32[]{:S(2)}) collective-permute-start(bf16[352,2048]{1,0:T(8,128)(2,1)} %convolution_convert_fusion.6), channel_id=1, source_target_pairs={{0,16},{16,0},{1,17},{17,1},{2,18},{18,2},{3,19},{19,3},{4,20},{20... | collective-permute-start | bytes 4325384 | tf_op jit(solution)/shard_map/ppermute | solution.py:759
  476.2 60.3 %collective-permute-start.57 = (bf16[128,2176]{1,0:T(8,128)(2,1)}, bf16[128,2176]{1,0:T(8,128)(2,1)}, u32[]{:S(2)}, u32[]{:S(2)}) collective-permute-start(bf16[128,2176]{1,0:T(8,128)(2,1)} %get-tuple-element.100), channel_id=1, source_target_pairs={{0,1},{1,0},{2,3},{3,2},{4,5},{5,4},{6,7},{7,6},{8,9},{9,8},{10,11... | collective-permute-start | bytes 1671176 | tf_op jit(solution)/shard_map/ppermute | solution.py:266
  536.6 67.2 %collective-permute-start.46 = (bf16[128,2176]{1,0:T(8,128)(2,1)}, bf16[128,2176]{1,0:T(8,128)(2,1)S(1)}, u32[]{:S(2)}, u32[]{:S(2)}) collective-permute-start(bf16[128,2176]{1,0:T(8,128)(2,1)} %get-tuple-element.99), channel_id=1, source_target_pairs={{0,1},{1,0},{2,3},{3,2},{4,5},{5,4},{6,7},{7,6},{8,9},{9,8},{10,11... | collective-permute-start | bytes 1671176 | tf_op jit(solution)/shard_map/ppermute | solution.py:266
  599.2 40.9 %collective-permute-start.83 = (bf16[16,64,352]{2,1,0:T(8,128)(2,1)}, bf16[16,64,352]{2,1,0:T(8,128)(2,1)}, u32[]{:S(2)}, u32[]{:S(2)}) collective-permute-start(bf16[16,64,352]{2,1,0:T(8,128)(2,1)} %fusion.29), channel_id=1, source_target_pairs={{0,16},{16,0},{1,17},{17,1},{2,18},{18,2},{3,19},{19,3},{4,20},{20... | collective-permute-start | bytes 2162696 | tf_op jit(solution)/shard_map/ppermute | solution.py:243
  602.1 76.9 %collective-permute-start.84 = (bf16[88,2048]{1,0:T(8,128)(2,1)}, bf16[88,2048]{1,0:T(8,128)(2,1)}, u32[]{:S(2)}, u32[]{:S(2)}) collective-permute-start(bf16[88,2048]{1,0:T(8,128)(2,1)} %fusion.37), channel_id=1, source_target_pairs={{0,16},{16,0},{1,17},{17,1},{2,18},{18,2},{3,19},{19,3},{4,20},{20... | collective-permute-start | bytes 1081352 | tf_op jit(solution)/shard_map/ppermute | solution.py:243
  633.8 49.1 %collective-permute-start.69 = (bf16[256,2816]{1,0:T(8,128)(2,1)}, bf16[256,2816]{1,0:T(8,128)(2,1)}, u32[]{:S(2)}, u32[]{:S(2)}) collective-permute-start(bf16[256,2816]{1,0:T(8,128)(2,1)} %convolution_convert_fusion.5), channel_id=1, source_target_pairs={{0,16},{16,0},{1,17},{17,1},{2,18},{18,2},{3,19},{19,3},{4,20},{20... | collective-permute-start | bytes 4325384 | tf_op jit(solution)/shard_map/ppermute | solution.py:759
  635.7 63.7 %collective-permute-start.72 = (bf16[256,2816]{1,0:T(8,128)(2,1)}, bf16[256,2816]{1,0:T(8,128)(2,1)}, u32[]{:S(2)}, u32[]{:S(2)}) collective-permute-start(bf16[256,2816]{1,0:T(8,128)(2,1)} %convolution_convert_fusion.4), channel_id=1, source_target_pairs={{0,16},{16,0},{1,17},{17,1},{2,18},{18,2},{3,19},{19,3},{4,20},{20... | collective-permute-start | bytes 4325384 | tf_op jit(solution)/shard_map/ppermute | solution.py:759
  642.4 58.8 %all-to-all-start.5 = ((bf16[16,64,352]{2,1,0:T(8,128)(2,1)}), bf16[16,64,352]{2,1,0:T(8,128)(2,1)}, u32[]{:S(2)}, u32[]{:S(2)}) async-start(bf16[16,64,352]{2,1,0:T(8,128)(2,1)} %fusion.13), calls=%async_computation.7 | async-start | bytes 1572864 | tf_op jit(solution)/shard_map/all_to_all | solution.py:573
  648.6 236.7 %reduce-scatter.5.cloned.1.call-start = ((), (), s32[]{:S(2)}) async-start(), calls=%async_computation.11 | async-start | bytes 8912896 | tf_op jit(solution)/shard_map/reduce_scatter | solution.py:814
  672.7 40.6 %collective-permute-start.67 = (bf16[128,2048]{1,0:T(8,128)(2,1)}, bf16[128,2048]{1,0:T(8,128)(2,1)}, u32[]{:S(2)}, u32[]{:S(2)}) collective-permute-start(bf16[128,2048]{1,0:T(8,128)(2,1)} %get-tuple-element.115), channel_id=1, source_target_pairs={{0,1},{1,0},{2,3},{3,2},{4,5},{5,4},{6,7},{7,6},{8,9},{9,8},{10,11... | collective-permute-start | bytes 1572872 | tf_op jit(solution)/shard_map/ppermute | solution.py:266
  679.0 198.1 %collective-permute-start.85 = (bf16[256,2816]{1,0:T(8,128)(2,1)}, bf16[256,2816]{1,0:T(8,128)(2,1)}, u32[]{:S(2)}, u32[]{:S(2)}) collective-permute-start(bf16[256,2816]{1,0:T(8,128)(2,1)} %convolution_convert_fusion.3), channel_id=1, source_target_pairs={{0,16},{16,0},{1,17},{17,1},{2,18},{18,2},{3,19},{19,3},{4,20},{20... | collective-permute-start | bytes 4325384 | tf_op jit(solution)/shard_map/ppermute | solution.py:759
  775.7 105.4 %collective-permute-start.86 = (bf16[256,2816]{1,0:T(8,128)(2,1)}, bf16[256,2816]{1,0:T(8,128)(2,1)}, u32[]{:S(2)}, u32[]{:S(2)}) collective-permute-start(bf16[256,2816]{1,0:T(8,128)(2,1)} %convolution_convert_fusion.2), channel_id=1, source_target_pairs={{0,16},{16,0},{1,17},{17,1},{2,18},{18,2},{3,19},{19,3},{4,20},{20... | collective-permute-start | bytes 4325384 | tf_op jit(solution)/shard_map/ppermute | solution.py:759
  778.9 78.6 %all-to-all-start.4 = ((bf16[16,64,512]{2,1,0:T(8,128)(2,1)}), bf16[16,64,512]{2,1,0:T(8,128)(2,1)S(1)}, u32[]{:S(2)}, u32[]{:S(2)}) async-start(bf16[16,64,512]{2,1,0:T(8,128)(2,1)} %fusion.9), calls=%async_computation.5 | async-start | bytes 2097152 | tf_op jit(solution)/shard_map/all_to_all | solution.py:573
  784.9 84.8 %collective-permute-start.63 = (bf16[128,2048]{1,0:T(8,128)(2,1)}, bf16[128,2048]{1,0:T(8,128)(2,1)}, u32[]{:S(2)}, u32[]{:S(2)}) collective-permute-start(bf16[128,2048]{1,0:T(8,128)(2,1)} %get-tuple-element.111), channel_id=1, source_target_pairs={{0,1},{1,0},{2,3},{3,2},{4,5},{5,4},{6,7},{7,6},{8,9},{9,8},{10,11... | collective-permute-start | bytes 1572872 | tf_op jit(solution)/shard_map/ppermute | solution.py:266
  785.4 42.1 %collective-permute-start.75 = (bf16[128,2048]{1,0:T(8,128)(2,1)}, bf16[128,2048]{1,0:T(8,128)(2,1)S(1)}, u32[]{:S(2)}, u32[]{:S(2)}) collective-permute-start(bf16[128,2048]{1,0:T(8,128)(2,1)} %get-tuple-element.113), channel_id=1, source_target_pairs={{0,1},{1,0},{2,3},{3,2},{4,5},{5,4},{6,7},{7,6},{8,9},{9,8},{10,11... | collective-permute-start | bytes 1572872 | tf_op jit(solution)/shard_map/ppermute | solution.py:266
  (154 other events, 2340.9 us)
Sparse Core Ops, SparseCore 0:
  18.8 96.6 all-gather.2
  117.7 91.1 all-gather.4
  429.3 144.2 reduce-scatter.2
  679.1 138.9 reduce-scatter.4

commit v2 on v1

--- a/solution.py
+++ b/solution.py
@@ -669,13 +669,14 @@
     mixed = mixed[:, :count].transpose(1, 0, 2).reshape(count, n_dp, n_e, rows)
     mixed = mixed.transpose(0, 2, 1, 3).reshape(count, width)
     share_w = swap(tied(share_w, lse))
-    proj_all = gather_all(dp_gather(attn_out).reshape(n_dp * rows, width))
+    proj_all = dp_gather(attn_out).reshape(n_dp * rows, width)
+    proj_all = gather_all(tied(proj_all, norm_blocks[-3][0], norm_blocks[-5][0]))
     routes_all = small[:, n_e + 1 : n_e + 1 + TOP].astype(F32)
     small = small[:, : n_e + 1].reshape(n_e, n_e + 1, n_dp, rows).transpose(1, 2, 0, 3)
     small = small.reshape(n_e + 1, width)
     router_full = small[:n_e]
     gain_second = small[n_e].astype(F32)
-    cot_all = gather_all(cotangent)
+    cot_all = gather_all(tied(cotangent, lse))
 
     share_sent = share_w
     share_w = dp_gather(share_w).reshape(width, 2 * shared_width)

time: 916 us -> 951 us (1.038)
  waiting for transfers between devices: 312 us -> 338 us
  starting transfers between devices: 126 us -> 136 us
    ppermute x6, waiting for transfers between devices: 58.6 us -> 98.7 us  [spread(): lax.ppermute(shard[j * size:(j + 1) * size], 'dp', [(i, (i - step) % n_dp...]
    ppermute x32, starting transfers between devices: 51.3 us -> 70.1 us  [ring_shift(): return lax.ppermute(value, 'expert', perm)]
    ppermute x5, waiting for transfers between devices: 19.5 us -> 3.55 us  [dp_gather(): lax.ppermute(value, 'dp', [(i, (i - step) % count) for i in range(count)])]
  transfers between devices with their start and end apart: 97 -> 97, of which waited for: 31 -> 36; matrix products, arithmetic and copies ran while one was open for 30% -> 29% of each run, Pallas kernels for 9% -> 9%
where the time goes in v2:
time: 951 us; the launch traced here: 940 us
  waiting for transfers between devices  338 us (36%)
  Pallas kernels  139 us (15%)
  starting transfers between devices  136 us (14%)
  matrix products  108 us (11%)
  local copies, waits for them, and re-layouts  96.7 us (10%)
  other arithmetic  90.8 us (10%)
  between operations  31.9 us (3%)
    ppermute x32, waiting for transfers between devices, ring_shift(): return lax.ppermute(value, 'expert', perm)  210 us
    ppermute x6, waiting for transfers between devices, spread(): lax.ppermute(shard[j * size:(j + 1) * size], 'dp', [(i, (i - step) % n_dp...  98.7 us
    dot_general x12, matrix products, dot_tn(): lax.dot_general(left, right, (((0,), (0,)), ((), ())), preferred_element_...  71.7 us
    ppermute x32, starting transfers between devices, ring_shift(): return lax.ppermute(value, 'expert', perm)  70.1 us
    pallas_call x1, Pallas kernels, expert(): pl.pallas_call(functools.partial(expert_kernel, len(ups)), out_shape=[jax...  46.1 us
    all_to_all x6, starting transfers between devices, swap(): lax.all_to_all(value, 'expert', split_axis=0, concat_axis=0, tiled=True)  37.2 us
    pallas_call x2, Pallas kernels, dispatch(): pl.pallas_call(functools.partial(dispatch_kernel, sources, tuple(widths),...  28.8 us
    pallas_call x1, Pallas kernels, attend(): pl.pallas_call(functools.partial(attend_kernel, sources, block), out_shap...  28.3 us
  transfers between devices with their start and end apart: 97, of which 36 were waited for; matrix products, arithmetic and copies ran while one was open for 29% of the time, Pallas kernels for 9%

profile of v2, /device:TPU:0, one launch (start us, length us, event | category | flops | bytes accessed | tf_op | source)
XLA Modules:
  0.0 939.9 jit_solution(4313032346652770617)
XLA Ops:
  16.0 7.4 all-to-all-start
  31.7 16.5 %collective-permute-done.1.refs_2_ = bf16[128,2048]{1,0:T(8,128)(2,1)S(1)} collective-permute-done((bf16[128,2048]{1,0:T(8,128)(2,1)S(1)}, bf16[128,2048]{1,0:T(8,128)(2,1)S(1)}, u32[]{:S(2)}, u32[]{:S(2)}) %collective-permute-start.1) | collective-permute-done | bytes 524320 | tf_op jit(solution)/shard_map/ppermute | solution.py:261
  54.2 7.9 collective-permute-done.9.refs_1_
  71.2 9.4 %collective-permute-done.10.refs_10_ = bf16[128,2048]{1,0:T(8,128)(2,1)S(1)} collective-permute-done((bf16[128,2048]{1,0:T(8,128)(2,1)S(1)}, bf16[128,2048]{1,0:T(8,128)(2,1)S(1)}, u32[]{:S(2)}, u32[]{:S(2)}) %collective-permute-start.10) | collective-permute-done | bytes 524320 | tf_op jit(solution)/shard_map/ppermute | solution.py:261
  123.9 9.1 collective-permute-done.17.refs_15_
  137.2 28.3 %attend.1 = (bf16[2048,128]{1,0:T(8,128)(2,1)S(1)}, bf16[2048,128]{1,0:T(8,128)(2,1)}, bf16[2048,128]{1,0:T(8,128)(2,1)}, bf16[2048,128]{1,0:T(8,128)(2,1)}, f32...) custom-call(s32[16]{0:T(128)S(1)} %fusion.63.order_ref.to_ref, bf16[128,2048]{1,0:T(8,128)(2,1)} %copy-done.40, ...), custom_call_target="tpu_custom_call" | custom-call | tf_op jit(solution)/shard_map/attend/pallas_call | solution.py:123
  169.8 32.5 %collective-permute-done.20.refs_2_ = bf16[256,2816]{1,0:T(8,128)(2,1)S(1)} collective-permute-done((bf16[256,2816]{1,0:T(8,128)(2,1)}, bf16[256,2816]{1,0:T(8,128)(2,1)S(1)}, u32[]{:S(2)}, u32[]{:S(2)}) %collective-permute-start.20) | collective-permute-done | bytes 1441824 | tf_op jit(solution)/shard_map/ppermute | solution.py:630
  217.9 23.1 %collective-permute-done.22.refs_3_ = bf16[256,2816]{1,0:T(8,128)(2,1)} collective-permute-done((bf16[256,2816]{1,0:T(8,128)(2,1)}, bf16[256,2816]{1,0:T(8,128)(2,1)}, u32[]{:S(2)}, u32[]{:S(2)}) %collective-permute-start.22) | collective-permute-done | bytes 1441824 | tf_op jit(solution)/shard_map/ppermute | solution.py:630
  267.1 35.3 %collective-permute-done.28.refs_4_ = bf16[256,2816]{1,0:T(8,128)(2,1)} collective-permute-done((bf16[256,2816]{1,0:T(8,128)(2,1)}, bf16[256,2816]{1,0:T(8,128)(2,1)}, u32[]{:S(2)}, u32[]{:S(2)}) %collective-permute-start.28) | collective-permute-done | bytes 1441824 | tf_op jit(solution)/shard_map/ppermute | solution.py:630
  307.6 12.1 %collective-permute-done.24.refs_2_ = bf16[128,2176]{1,0:T(8,128)(2,1)S(1)} collective-permute-done((bf16[128,2176]{1,0:T(8,128)(2,1)S(1)}, bf16[128,2176]{1,0:T(8,128)(2,1)S(1)}, u32[]{:S(2)}, u32[]{:S(2)}) %collective-permute-start.24) | collective-permute-done | bytes 557088 | tf_op jit(solution)/shard_map/ppermute | solution.py:261
  336.1 14.4 %collective-permute-done.33.refs_10_ = bf16[128,2176]{1,0:T(8,128)(2,1)S(1)} collective-permute-done((bf16[128,2176]{1,0:T(8,128)(2,1)}, bf16[128,2176]{1,0:T(8,128)(2,1)S(1)}, u32[]{:S(2)}, u32[]{:S(2)}) %collective-permute-start.33) | collective-permute-done | bytes 557088 | tf_op jit(solution)/shard_map/ppermute | solution.py:261
  363.6 14.2 %dispatch.2 = (bf16[2048,2048]{1,0:T(8,128)(2,1)}, bf16[2048,128]{1,0:T(8,128)(2,1)S(1)}, bf16[1280,2048]{1,0:T(8,128)(2,1)}, f32[1280,1]{1,0:T(8,128)}) custom-call(s32[16]{0:T(128)S(1)} %fusion.62.base_ref, s32[16]{0:T(128)S(1)} %fusion.63.order_ref.to_ref, s32[16,1,128]{2,1,0:T(1,128)S(1)} %fusion.48.pos_ref, ...), custom_call_target="tpu_custom_call" | custom-call | tf_op jit(solution)/shard_map/dispatch/pallas_call | solution.py:415
  377.8 8.6 fusion.72
  386.6 14.6 %dispatch.3 = (bf16[1280,2048]{1,0:T(8,128)(2,1)}, f32[1280,1]{1,0:T(8,128)S(1)}) custom-call(s32[16]{0:T(128)S(1)} %fusion.62.base_ref, s32[16]{0:T(128)S(1)} %fusion.63.order_ref.to_ref, s32[16,1,128]{2,1,0:T(1,128)S(1)} %fusion.48.pos_ref, f32[16,1,128]{2,1,0:T(1,128)S(1)} %bitcast.219, bf16[2048,2048]{1,0:T(8,128)(2,1)} %all-gather.5.cloned.1.call-done.refs_0_), custom_call_target="tpu_custom_call" | custom-call | tf_op jit(solution)/shard_map/dispatch/pallas_call | solution.py:415
  401.2 8.4 multiply_convert_fusion.1
  409.6 46.1 %expert.1 = (bf16[1280,2048]{1,0:T(8,128)(2,1)}, bf16[1280,2048]{1,0:T(8,128)(2,1)}, bf16[1280,1408]{1,0:T(8,128)(2,1)}, bf16[1280,2048]{1,0:T(8,128)(2,1)}, bf1...) custom-call(s32[1]{0:T(128)} %bitcast.38.total_ref, s32[8]{0:T(128)} %stack.89.starts_ref, ...), custom_call_target="tpu_custom_call" | custom-call | tf_op jit(solution)/shard_map/expert/pallas_call | solution.py:498
  458.3 10.9 %combine.2 = bf16[2048,2048]{1,0:T(8,128)(2,1)} custom-call(s32[16]{0:T(128)S(1)} %fusion.62.base_ref, s32[16]{0:T(128)S(1)} %fusion.63.order_ref.to_ref, s32[16]{0:T(128)S(1)} %fusion.63.order_ref.to_ref, s32[1]{0:T(128)} %bitcast.35.me_ref, s32[16,1,128]{2,1,0:T(1,128)S(1)} %fusion.48.pos_ref, bf16[1280,2048]{1,0:T(8,128)(2,1)S(1)} %copy-done.3, ...), custom_call_target="tpu_custom_call" | custom-call | tf_op jit(solution)/shard_map/combine/pallas_call | solution.py:546
  473.9 14.0 %combine.3 = bf16[2048,2176]{1,0:T(8,128)(2,1)} custom-call(s32[16]{0:T(128)S(1)} %fusion.62.base_ref, s32[16]{0:T(128)S(1)} %fusion.63.order_ref.to_ref, s32[16]{0:T(128)S(1)} %iota.41.to_ref, s32[1]{0:T(128)} %bitcast.35.me_ref, s32[16,1,128]{2,1,0:T(1,128)S(1)} %fusion.48.pos_ref, bf16[1280,2048]{1,0:T(8,128)(2,1)S(1)} %copy-done.2, ...), custom_call_target="tpu_custom_call" | custom-call | tf_op jit(solution)/shard_map/combine/pallas_call | solution.py:546
  500.0 7.4 convolution_convert_fusion.6
  509.4 16.9 %collective-permute-start.51 = (bf16[64,2176]{1,0:T(8,128)(2,1)S(1)}, bf16[64,2176]{1,0:T(8,128)(2,1)S(1)}, u32[]{:S(2)}, u32[]{:S(2)}) collective-permute-start(bf16[64,2176]{1,0:T(8,128)(2,1)S(1)} %get-tuple-element.146), channel_id=1, source_target_pairs={{0,4},{1,5},{4,8},{5,9},{8,12},{9,13},{12,14},{13,15},{14,10},{15,... | collective-permute-start | bytes 835592 | tf_op jit(solution)/shard_map/ppermute | solution.py:261
  526.4 10.9 %convolution_bitcast_fusion = f32[1,1024,2816]{2,1,0:T(8,128)} fusion(bf16[1280,2816]{1,0:T(8,128)(2,1)S(1)} %bitcast.221, bf16[1280,2048]{1,0:T(8,128)(2,1)S(1)} %bitcast.232, s32[]{:T(128)S(6)} %select_n.235), kind=kOutput, calls=%fused_computation.3 | convolution fusion | flops 7381975040 | bytes 21364740 | tf_op jit(solution)/shard_map/dot_general | solution.py:54
  545.0 7.1 fusion.74
  552.2 16.4 %collective-permute-done.52 = bf16[128,2176]{1,0:T(8,128)(2,1)S(1)} collective-permute-done((bf16[128,2176]{1,0:T(8,128)(2,1)}, bf16[128,2176]{1,0:T(8,128)(2,1)S(1)}, u32[]{:S(2)}, u32[]{:S(2)}) %collective-permute-start.52) | collective-permute-done | bytes 557088 | tf_op jit(solution)/shard_map/ppermute | solution.py:261
  575.6 12.9 %collective-permute-done.53 = bf16[128,2176]{1,0:T(8,128)(2,1)S(1)} collective-permute-done((bf16[128,2176]{1,0:T(8,128)(2,1)S(1)}, bf16[128,2176]{1,0:T(8,128)(2,1)S(1)}, u32[]{:S(2)}, u32[]{:S(2)}) %collective-permute-start.53) | collective-permute-done | bytes 557088 | tf_op jit(solution)/shard_map/ppermute | solution.py:261
  594.2 13.3 %collective-permute-done.58 = bf16[64,2176]{1,0:T(8,128)(2,1)S(1)} collective-permute-done((bf16[64,2176]{1,0:T(8,128)(2,1)S(1)}, bf16[64,2176]{1,0:T(8,128)(2,1)S(1)}, u32[]{:S(2)}, u32[]{:S(2)}) %collective-permute-start.58) | collective-permute-done | bytes 278560 | tf_op jit(solution)/shard_map/ppermute | solution.py:261
  607.7 9.2 convolution_bitcast_fusion.1
  691.2 10.8 %attend_back.1 = bf16[2048,384]{1,0:T(8,128)(2,1)S(1)} custom-call(s32[16]{0:T(128)S(1)} %fusion.63.order_ref.to_ref, bf16[2048,128]{1,0:T(8,128)(2,1)S(1)} %copy-done.9, bf16[2048,128]{1,0:T(8,128)(2,1)S(1)} %copy-done.10, bf16[2048,128]{1,0:T(8,128)(2,1)S(1)} %copy-done.11, bf16[2048,128]{1,0:T(8,128)(2,1)S(1)} %bitcast.214, ...), custom_call_target="tpu_custom_call" | custom-call | tf_op jit(solution)/shard_map/attend_back/pallas_call | solution.py:201
  723.3 15.2 %collective-permute-done.72 = bf16[256,2816]{1,0:T(8,128)(2,1)} collective-permute-done((bf16[256,2816]{1,0:T(8,128)(2,1)}, bf16[256,2816]{1,0:T(8,128)(2,1)}, u32[]{:S(2)}, u32[]{:S(2)}) %collective-permute-start.72) | collective-permute-done | bytes 1441824 | tf_op jit(solution)/shard_map/ppermute | solution.py:760
  760.4 8.8 collective-permute-done.68
  829.1 31.2 %collective-permute-done.77 = bf16[64,2048]{1,0:T(8,128)(2,1)S(1)} collective-permute-done((bf16[64,2048]{1,0:T(8,128)(2,1)S(1)}, bf16[64,2048]{1,0:T(8,128)(2,1)S(1)}, u32[]{:S(2)}, u32[]{:S(2)}) %collective-permute-start.77) | collective-permute-done | bytes 262176 | tf_op jit(solution)/shard_map/ppermute | solution.py:261
  866.2 13.6 %collective-permute-done.78 = bf16[128,2048]{1,0:T(8,128)(2,1)S(1)} collective-permute-done((bf16[128,2048]{1,0:T(8,128)(2,1)S(1)}, bf16[128,2048]{1,0:T(8,128)(2,1)S(1)}, u32[]{:S(2)}, u32[]{:S(2)}) %collective-permute-start.78) | collective-permute-done | bytes 524320 | tf_op jit(solution)/shard_map/ppermute | solution.py:261
  884.1 10.4 %collective-permute-done.79 = bf16[128,2048]{1,0:T(8,128)(2,1)S(1)} collective-permute-done((bf16[128,2048]{1,0:T(8,128)(2,1)S(1)}, bf16[128,2048]{1,0:T(8,128)(2,1)S(1)}, u32[]{:S(2)}, u32[]{:S(2)}) %collective-permute-start.79) | collective-permute-done | bytes 524320 | tf_op jit(solution)/shard_map/ppermute | solution.py:261
  (583 shorter events, 411.1 us)
Async XLA Ops:
  16.0 47.8 %all-to-all-start = ((bf16[16,64,384]{2,1,0:T(8,128)(2,1)}), bf16[16,64,384]{2,1,0:T(8,128)(2,1)}, u32[]{:S(2)}, u32[]{:S(2)}) async-start(bf16[16,64,384]{2,1,0:T(8,128)(2,1)} %reshape.448), calls=%async_computation | async-start | bytes 1572864 | tf_op jit(solution)/shard_map/all_to_all | solution.py:573
  23.3 231.7 %all-gather.3.cloned.1.call-start = ((), (), s32[]{:S(2)}) async-start(), calls=%async_computation.8 | async-start | bytes 8912896 | tf_op jit(solution)/shard_map/all_gather | solution.py:569
  86.8 299.8 %all-gather.5.cloned.1.call-start = ((), (), s32[]{:S(2)}) async-start(), calls=%async_computation.9 | async-start | bytes 8912896 | tf_op jit(solution)/shard_map/all_gather | solution.py:569
  167.6 97.7 %collective-permute-start.44 = (bf16[88,2048]{1,0:T(8,128)(2,1)}, bf16[88,2048]{1,0:T(8,128)(2,1)}, u32[]{:S(2)}, u32[]{:S(2)}) collective-permute-start(bf16[88,2048]{1,0:T(8,128)(2,1)} %param.22), channel_id=1, source_target_pairs={{0,16},{16,0},{1,17},{17,1},{2,18},{18,2},{3,19},{19,3},{4,20},{20... | collective-permute-start | bytes 1081352 | tf_op jit(solution)/shard_map/ppermute | solution.py:223
  169.7 71.3 %collective-permute-start.22 = (bf16[256,2816]{1,0:T(8,128)(2,1)}, bf16[256,2816]{1,0:T(8,128)(2,1)}, u32[]{:S(2)}, u32[]{:S(2)}) collective-permute-start(bf16[256,2816]{1,0:T(8,128)(2,1)} %get-tuple-element.124), channel_id=1, source_target_pairs={{0,16},{16,0},{1,17},{17,1},{2,18},{18,2},{3,19},{19,3},{4,20},{20... | collective-permute-start | bytes 4325384 | tf_op jit(solution)/shard_map/ppermute | solution.py:630
  205.5 39.5 %all-to-all-start.1 = ((bf16[16,160,128]{2,1,0:T(8,128)(2,1)}), bf16[16,160,128]{2,1,0:T(8,128)(2,1)}, u32[]{:S(2)}, u32[]{:S(2)}) async-start(bf16[16,160,128]{2,1,0:T(8,128)(2,1)} %multiply_convert_fusion.4), calls=%async_computation.1 | async-start | bytes 1310720 | tf_op jit(solution)/shard_map/all_to_all | solution.py:573
  213.7 109.1 %collective-permute-start.37 = (bf16[352,2048]{1,0:T(8,128)(2,1)}, bf16[352,2048]{1,0:T(8,128)(2,1)}, u32[]{:S(2)}, u32[]{:S(2)}) collective-permute-start(bf16[352,2048]{1,0:T(8,128)(2,1)} %get-tuple-element.131), channel_id=1, source_target_pairs={{0,16},{16,0},{1,17},{17,1},{2,18},{18,2},{3,19},{19,3},{4,20},{20... | collective-permute-start | bytes 4325384 | tf_op jit(solution)/shard_map/ppermute | solution.py:630
  213.8 88.6 %collective-permute-start.28 = (bf16[256,2816]{1,0:T(8,128)(2,1)}, bf16[256,2816]{1,0:T(8,128)(2,1)}, u32[]{:S(2)}, u32[]{:S(2)}) collective-permute-start(bf16[256,2816]{1,0:T(8,128)(2,1)} %get-tuple-element.123), channel_id=1, source_target_pairs={{0,16},{16,0},{1,17},{17,1},{2,18},{18,2},{3,19},{19,3},{4,20},{20... | collective-permute-start | bytes 4325384 | tf_op jit(solution)/shard_map/ppermute | solution.py:630
  245.0 58.5 %all-to-all-start.2 = ((bf16[16,64,352]{2,1,0:T(8,128)(2,1)}), bf16[16,64,352]{2,1,0:T(8,128)(2,1)S(1)}, u32[]{:S(2)}, u32[]{:S(2)}) async-start(bf16[16,64,352]{2,1,0:T(8,128)(2,1)} %multiply_convert_fusion.3), calls=%async_computation.2 | async-start | bytes 1572864 | tf_op jit(solution)/shard_map/all_to_all | solution.py:573
  251.8 398.9 %reduce-scatter.3.cloned.1.call-start = ((), (), s32[]{:S(2)}) async-start(), calls=%async_computation.10 | async-start | bytes 8912896 | tf_op jit(solution)/shard_map/reduce_scatter | solution.py:752
  262.6 42.8 %collective-permute-start.26 = (bf16[128,2176]{1,0:T(8,128)(2,1)S(1)}, bf16[128,2176]{1,0:T(8,128)(2,1)S(1)}, u32[]{:S(2)}, u32[]{:S(2)}) collective-permute-start(bf16[128,2176]{1,0:T(8,128)(2,1)S(1)} %concatenate.54.refs_0_), channel_id=1, source_target_pairs={{0,2},{1,3},{4,0},{5,1},{8,4},{9,5},{12,8},{13,9},{14,12},{15,13},... | collective-permute-start | bytes 1671176 | tf_op jit(solution)/shard_map/ppermute | solution.py:261
  361.8 47.9 %collective-permute-start.42 = (bf16[352,2048]{1,0:T(8,128)(2,1)}, bf16[352,2048]{1,0:T(8,128)(2,1)}, u32[]{:S(2)}, u32[]{:S(2)}) collective-permute-start(bf16[352,2048]{1,0:T(8,128)(2,1)} %get-tuple-element.130), channel_id=1, source_target_pairs={{0,16},{16,0},{1,17},{17,1},{2,18},{18,2},{3,19},{19,3},{4,20},{20... | collective-permute-start | bytes 4325384 | tf_op jit(solution)/shard_map/ppermute | solution.py:630
  499.2 140.7 %collective-permute-start.45 = (bf16[352,2048]{1,0:T(8,128)(2,1)}, bf16[352,2048]{1,0:T(8,128)(2,1)S(1)}, u32[]{:S(2)}, u32[]{:S(2)}) collective-permute-start(bf16[352,2048]{1,0:T(8,128)(2,1)} %convolution_convert_fusion.7), channel_id=1, source_target_pairs={{0,16},{16,0},{1,17},{17,1},{2,18},{18,2},{3,19},{19,3},{4,20},{20... | collective-permute-start | bytes 4325384 | tf_op jit(solution)/shard_map/ppermute | solution.py:760
  507.5 135.1 %collective-permute-start.62 = (bf16[352,2048]{1,0:T(8,128)(2,1)}, bf16[352,2048]{1,0:T(8,128)(2,1)S(1)}, u32[]{:S(2)}, u32[]{:S(2)}) collective-permute-start(bf16[352,2048]{1,0:T(8,128)(2,1)} %convolution_convert_fusion.6), channel_id=1, source_target_pairs={{0,16},{16,0},{1,17},{17,1},{2,18},{18,2},{3,19},{19,3},{4,20},{20... | collective-permute-start | bytes 4325384 | tf_op jit(solution)/shard_map/ppermute | solution.py:760
  508.6 66.5 %collective-permute-start.57 = (bf16[128,2176]{1,0:T(8,128)(2,1)}, bf16[128,2176]{1,0:T(8,128)(2,1)}, u32[]{:S(2)}, u32[]{:S(2)}) collective-permute-start(bf16[128,2176]{1,0:T(8,128)(2,1)} %get-tuple-element.100), channel_id=1, source_target_pairs={{0,1},{1,0},{2,3},{3,2},{4,5},{5,4},{6,7},{7,6},{8,9},{9,8},{10,11... | collective-permute-start | bytes 1671176 | tf_op jit(solution)/shard_map/ppermute | solution.py:266
  508.6 43.5 %collective-permute-start.48 = (bf16[128,2176]{1,0:T(8,128)(2,1)}, bf16[128,2176]{1,0:T(8,128)(2,1)}, u32[]{:S(2)}, u32[]{:S(2)}) collective-permute-start(bf16[128,2176]{1,0:T(8,128)(2,1)} %get-tuple-element.105), channel_id=1, source_target_pairs={{0,1},{1,0},{2,3},{3,2},{4,5},{5,4},{6,7},{7,6},{8,9},{9,8},{10,11... | collective-permute-start | bytes 1671176 | tf_op jit(solution)/shard_map/ppermute | solution.py:266
  575.1 69.3 %collective-permute-start.46 = (bf16[128,2176]{1,0:T(8,128)(2,1)}, bf16[128,2176]{1,0:T(8,128)(2,1)S(1)}, u32[]{:S(2)}, u32[]{:S(2)}) collective-permute-start(bf16[128,2176]{1,0:T(8,128)(2,1)} %get-tuple-element.99), channel_id=1, source_target_pairs={{0,1},{1,0},{2,3},{3,2},{4,5},{5,4},{6,7},{7,6},{8,9},{9,8},{10,11... | collective-permute-start | bytes 1671176 | tf_op jit(solution)/shard_map/ppermute | solution.py:266
  575.1 41.8 %collective-permute-start.56 = (bf16[128,2176]{1,0:T(8,128)(2,1)S(1)}, bf16[128,2176]{1,0:T(8,128)(2,1)S(1)}, u32[]{:S(2)}, u32[]{:S(2)}) collective-permute-start(bf16[128,2176]{1,0:T(8,128)(2,1)S(1)} %get-tuple-element.101), channel_id=1, source_target_pairs={{0,1},{1,0},{2,3},{3,2},{4,5},{5,4},{6,7},{7,6},{8,9},{9,8},{10,11... | collective-permute-start | bytes 1671176 | tf_op jit(solution)/shard_map/ppermute | solution.py:266
  639.9 39.3 %collective-permute-start.83 = (bf16[16,64,352]{2,1,0:T(8,128)(2,1)}, bf16[16,64,352]{2,1,0:T(8,128)(2,1)}, u32[]{:S(2)}, u32[]{:S(2)}) collective-permute-start(bf16[16,64,352]{2,1,0:T(8,128)(2,1)} %fusion.31), channel_id=1, source_target_pairs={{0,16},{16,0},{1,17},{17,1},{2,18},{18,2},{3,19},{19,3},{4,20},{20... | collective-permute-start | bytes 2162696 | tf_op jit(solution)/shard_map/ppermute | solution.py:243
  642.6 75.4 %collective-permute-start.84 = (bf16[88,2048]{1,0:T(8,128)(2,1)}, bf16[88,2048]{1,0:T(8,128)(2,1)}, u32[]{:S(2)}, u32[]{:S(2)}) collective-permute-start(bf16[88,2048]{1,0:T(8,128)(2,1)} %fusion.39), channel_id=1, source_target_pairs={{0,16},{16,0},{1,17},{17,1},{2,18},{18,2},{3,19},{19,3},{4,20},{20... | collective-permute-start | bytes 1081352 | tf_op jit(solution)/shard_map/ppermute | solution.py:243
  672.9 48.6 %collective-permute-start.69 = (bf16[256,2816]{1,0:T(8,128)(2,1)}, bf16[256,2816]{1,0:T(8,128)(2,1)}, u32[]{:S(2)}, u32[]{:S(2)}) collective-permute-start(bf16[256,2816]{1,0:T(8,128)(2,1)} %convolution_convert_fusion.5), channel_id=1, source_target_pairs={{0,16},{16,0},{1,17},{17,1},{2,18},{18,2},{3,19},{19,3},{4,20},{20... | collective-permute-start | bytes 4325384 | tf_op jit(solution)/shard_map/ppermute | solution.py:760
  674.3 64.2 %collective-permute-start.72 = (bf16[256,2816]{1,0:T(8,128)(2,1)}, bf16[256,2816]{1,0:T(8,128)(2,1)}, u32[]{:S(2)}, u32[]{:S(2)}) collective-permute-start(bf16[256,2816]{1,0:T(8,128)(2,1)} %convolution_convert_fusion.4), channel_id=1, source_target_pairs={{0,16},{16,0},{1,17},{17,1},{2,18},{18,2},{3,19},{19,3},{4,20},{20... | collective-permute-start | bytes 4325384 | tf_op jit(solution)/shard_map/ppermute | solution.py:760
  681.5 58.8 %all-to-all-start.5 = ((bf16[16,64,352]{2,1,0:T(8,128)(2,1)}), bf16[16,64,352]{2,1,0:T(8,128)(2,1)}, u32[]{:S(2)}, u32[]{:S(2)}) async-start(bf16[16,64,352]{2,1,0:T(8,128)(2,1)} %fusion.13), calls=%async_computation.7 | async-start | bytes 1572864 | tf_op jit(solution)/shard_map/all_to_all | solution.py:573
  687.6 236.3 %reduce-scatter.5.cloned.1.call-start = ((), (), s32[]{:S(2)}) async-start(), calls=%async_computation.11 | async-start | bytes 8912896 | tf_op jit(solution)/shard_map/reduce_scatter | solution.py:815
  711.8 40.7 %collective-permute-start.67 = (bf16[128,2048]{1,0:T(8,128)(2,1)}, bf16[128,2048]{1,0:T(8,128)(2,1)}, u32[]{:S(2)}, u32[]{:S(2)}) collective-permute-start(bf16[128,2048]{1,0:T(8,128)(2,1)} %get-tuple-element.115), channel_id=1, source_target_pairs={{0,1},{1,0},{2,3},{3,2},{4,5},{5,4},{6,7},{7,6},{8,9},{9,8},{10,11... | collective-permute-start | bytes 1572872 | tf_op jit(solution)/shard_map/ppermute | solution.py:266
  712.1 40.4 %collective-permute-start.66 = (bf16[128,2048]{1,0:T(8,128)(2,1)}, bf16[128,2048]{1,0:T(8,128)(2,1)}, u32[]{:S(2)}, u32[]{:S(2)}) collective-permute-start(bf16[128,2048]{1,0:T(8,128)(2,1)} %get-tuple-element.116), channel_id=1, source_target_pairs={{0,1},{1,0},{2,3},{3,2},{4,5},{5,4},{6,7},{7,6},{8,9},{9,8},{10,11... | collective-permute-start | bytes 1572872 | tf_op jit(solution)/shard_map/ppermute | solution.py:266
  718.0 197.7 %collective-permute-start.85 = (bf16[256,2816]{1,0:T(8,128)(2,1)}, bf16[256,2816]{1,0:T(8,128)(2,1)}, u32[]{:S(2)}, u32[]{:S(2)}) collective-permute-start(bf16[256,2816]{1,0:T(8,128)(2,1)} %convolution_convert_fusion.3), channel_id=1, source_target_pairs={{0,16},{16,0},{1,17},{17,1},{2,18},{18,2},{3,19},{19,3},{4,20},{20... | collective-permute-start | bytes 4325384 | tf_op jit(solution)/shard_map/ppermute | solution.py:760
  814.6 105.2 %collective-permute-start.86 = (bf16[256,2816]{1,0:T(8,128)(2,1)}, bf16[256,2816]{1,0:T(8,128)(2,1)}, u32[]{:S(2)}, u32[]{:S(2)}) collective-permute-start(bf16[256,2816]{1,0:T(8,128)(2,1)} %convolution_convert_fusion.2), channel_id=1, source_target_pairs={{0,16},{16,0},{1,17},{17,1},{2,18},{18,2},{3,19},{19,3},{4,20},{20... | collective-permute-start | bytes 4325384 | tf_op jit(solution)/shard_map/ppermute | solution.py:760
  817.5 78.5 %all-to-all-start.4 = ((bf16[16,64,512]{2,1,0:T(8,128)(2,1)}), bf16[16,64,512]{2,1,0:T(8,128)(2,1)S(1)}, u32[]{:S(2)}, u32[]{:S(2)}) async-start(bf16[16,64,512]{2,1,0:T(8,128)(2,1)} %fusion.9), calls=%async_computation.5 | async-start | bytes 2097152 | tf_op jit(solution)/shard_map/all_to_all | solution.py:573
  823.7 84.7 %collective-permute-start.63 = (bf16[128,2048]{1,0:T(8,128)(2,1)}, bf16[128,2048]{1,0:T(8,128)(2,1)}, u32[]{:S(2)}, u32[]{:S(2)}) collective-permute-start(bf16[128,2048]{1,0:T(8,128)(2,1)} %get-tuple-element.111), channel_id=1, source_target_pairs={{0,1},{1,0},{2,3},{3,2},{4,5},{5,4},{6,7},{7,6},{8,9},{9,8},{10,11... | collective-permute-start | bytes 1572872 | tf_op jit(solution)/shard_map/ppermute | solution.py:266
  824.2 41.9 %collective-permute-start.75 = (bf16[128,2048]{1,0:T(8,128)(2,1)}, bf16[128,2048]{1,0:T(8,128)(2,1)S(1)}, u32[]{:S(2)}, u32[]{:S(2)}) collective-permute-start(bf16[128,2048]{1,0:T(8,128)(2,1)} %get-tuple-element.113), channel_id=1, source_target_pairs={{0,1},{1,0},{2,3},{3,2},{4,5},{5,4},{6,7},{7,6},{8,9},{9,8},{10,11... | collective-permute-start | bytes 1572872 | tf_op jit(solution)/shard_map/ppermute | solution.py:266
  824.3 36.1 %collective-permute-start.77 = (bf16[64,2048]{1,0:T(8,128)(2,1)S(1)}, bf16[64,2048]{1,0:T(8,128)(2,1)S(1)}, u32[]{:S(2)}, u32[]{:S(2)}) collective-permute-start(bf16[64,2048]{1,0:T(8,128)(2,1)S(1)} %copy-done.78), channel_id=1, source_target_pairs={{0,2},{1,3},{4,0},{5,1},{8,4},{9,5},{12,8},{13,9},{14,12},{15,13},... | collective-permute-start | bytes 786440 | tf_op jit(solution)/shard_map/ppermute | solution.py:261
  (168 other events, 2454.1 us)
Sparse Core Ops, SparseCore 0:
  86.9 74.6 all-gather.2
  167.7 87.2 all-gather.4
  469.3 138.5 reduce-scatter.2
  718.2 138.2 reduce-scatter.4

commit v3 on v1

--- a/solution.py
+++ b/solution.py
@@ -654,7 +654,7 @@
     norm_blocks = ring_gather(
         normed_one.astype(BF16),
         {
-            half - 1: lambda blocks: [head_sent(blocks)] + up_tokens[0],
+            half - 1: lambda blocks: [head_sent(blocks)],
             half: lambda blocks: [head_whole(blocks), cos_table, sin_table, extra, share_w],
         },
     )
@@ -664,7 +664,7 @@
         norm_blocks, order, head_w, cos_table, sin_table, first_place
     )
     mixed = jnp.concatenate([head_out.reshape(n_e, count, HEAD_DIM), extra], axis=1)
-    mixed = swap(tied(mixed, *up_tokens[1]) if up_tokens[1] else mixed)
+    mixed = swap(tied(mixed, *up_tokens[0], *up_tokens[1]) if up_tokens[0] else mixed)
     small = mixed[:, count:]
     mixed = mixed[:, :count].transpose(1, 0, 2).reshape(count, n_dp, n_e, rows)
     mixed = mixed.transpose(0, 2, 1, 3).reshape(count, width)
@@ -699,8 +699,8 @@
     norm_blocks = ring_gather(
         payload,
         {
-            half - 2: lambda blocks: [share_sent] + up_tokens[3],
-            half: lambda blocks: first(down_parts[1]),
+            half - 1: lambda blocks: [share_sent],
+            half: lambda blocks: up_tokens[3] + [share_sent],
         },
     )
 

time: 916 us -> 919 us (level)
  waiting for transfers between devices: 312 us -> 292 us
  Pallas kernels: 140 us -> 156 us
  starting transfers between devices: 126 us -> 140 us
    ppermute x6, waiting for transfers between devices: 58.6 us -> 16.4 us  [spread(): lax.ppermute(shard[j * size:(j + 1) * size], 'dp', [(i, (i - step) % n_dp...]
    ppermute x32, starting transfers between devices: 51.3 us -> 70.8 us  [ring_shift(): return lax.ppermute(value, 'expert', perm)]
    pallas_call x1, Pallas kernels: 46.1 us -> 63.3 us  [expert(): pl.pallas_call(functools.partial(expert_kernel, len(ups)), out_shape=[jax...]
    ppermute x32, waiting for transfers between devices: 204 us -> 220 us  [ring_shift(): return lax.ppermute(value, 'expert', perm)]
  transfers between devices with their start and end apart: 97 -> 97, of which waited for: 31 -> 32; matrix products, arithmetic and copies ran while one was open for 30% -> 30% of each run, Pallas kernels for 9% -> 9%
where the time goes in v3:
time: 919 us; the launch traced here: 909 us
  waiting for transfers between devices  292 us (32%)
  Pallas kernels  156 us (17%)
  starting transfers between devices  140 us (15%)
  matrix products  108 us (12%)
  local copies, waits for them, and re-layouts  97.2 us (11%)
  other arithmetic  85 us (9%)
  between operations  30.4 us (3%)
    ppermute x32, waiting for transfers between devices, ring_shift(): return lax.ppermute(value, 'expert', perm)  220 us
    dot_general x12, matrix products, dot_tn(): lax.dot_general(left, right, (((0,), (0,)), ((), ())), preferred_element_...  72.1 us
    ppermute x32, starting transfers between devices, ring_shift(): return lax.ppermute(value, 'expert', perm)  70.8 us
    pallas_call x1, Pallas kernels, expert(): pl.pallas_call(functools.partial(expert_kernel, len(ups)), out_shape=[jax...  63.3 us
    all_to_all x6, starting transfers between devices, swap(): lax.all_to_all(value, 'expert', split_axis=0, concat_axis=0, tiled=True)  33.3 us
    pallas_call x2, Pallas kernels, dispatch(): pl.pallas_call(functools.partial(dispatch_kernel, sources, tuple(widths),...  28.8 us
    pallas_call x1, Pallas kernels, attend(): pl.pallas_call(functools.partial(attend_kernel, sources, block), out_shap...  28.4 us
    pallas_call x2, Pallas kernels, combine(): pl.pallas_call(functools.partial(combine_kernel, turned, window, extra),...  25 us
  transfers between devices with their start and end apart: 97, of which 32 were waited for; matrix products, arithmetic and copies ran while one was open for 30% of the time, Pallas kernels for 9%

profile of v3, /device:TPU:0, one launch (start us, length us, event | category | flops | bytes accessed | tf_op | source)
XLA Modules:
  0.0 908.7 jit_solution(14106185413372061522)
XLA Ops:
  69.8 10.7 %collective-permute-done.7.refs_8_ = bf16[128,2048]{1,0:T(8,128)(2,1)} collective-permute-done((bf16[128,2048]{1,0:T(8,128)(2,1)}, bf16[128,2048]{1,0:T(8,128)(2,1)}, u32[]{:S(2)}, u32[]{:S(2)}) %collective-permute-start.7) | collective-permute-done | bytes 524320 | tf_op jit(solution)/shard_map/ppermute | solution.py:261
  83.9 9.4 %collective-permute-start.11 = (bf16[128,2048]{1,0:T(8,128)(2,1)}, bf16[128,2048]{1,0:T(8,128)(2,1)}, u32[]{:S(2)}, u32[]{:S(2)}) collective-permute-start(bf16[128,2048]{1,0:T(8,128)(2,1)} %multiply_convert_fusion.10), channel_id=1, source_target_pairs={{0,2},{1,3},{4,0},{5,1},{8,4},{9,5},{12,8},{13,9},{14,12},{15,13},... | collective-permute-start | bytes 1572872 | tf_op jit(solution)/shard_map/ppermute | solution.py:261
  93.4 18.0 %collective-permute-done.13 = bf16[16,64,384]{2,1,0:T(8,128)(2,1)S(1)} collective-permute-done((bf16[16,64,384]{2,1,0:T(8,128)(2,1)}, bf16[16,64,384]{2,1,0:T(8,128)(2,1)S(1)}, u32[]{:S(2)}, u32[]{:S(2)}) %collective-permute-start.13) | collective-permute-done | bytes 786464 | tf_op jit(solution)/shard_map/ppermute | solution.py:223
  111.4 7.1 collective-permute-start.9
  145.2 9.1 %collective-permute-done.16.refs_15_ = bf16[64,2048]{1,0:T(8,128)(2,1)S(1)} collective-permute-done((bf16[64,2048]{1,0:T(8,128)(2,1)S(1)}, bf16[64,2048]{1,0:T(8,128)(2,1)S(1)}, u32[]{:S(2)}, u32[]{:S(2)}) %collective-permute-start.16) | collective-permute-done | bytes 262176 | tf_op jit(solution)/shard_map/ppermute | solution.py:261
  161.5 28.4 %attend.1 = (bf16[2048,128]{1,0:T(8,128)(2,1)S(1)}, bf16[2048,128]{1,0:T(8,128)(2,1)}, bf16[2048,128]{1,0:T(8,128)(2,1)}, bf16[2048,128]{1,0:T(8,128)(2,1)}, f32...) custom-call(s32[16]{0:T(128)S(1)} %fusion.61.order_ref.to_ref, bf16[128,2048]{1,0:T(8,128)(2,1)} %fusion.16.refs_0_, ...), custom_call_target="tpu_custom_call" | custom-call | tf_op jit(solution)/shard_map/attend/pallas_call | solution.py:123
  206.2 7.1 all-to-all-done.1
  231.0 15.7 %collective-permute-done.26.refs_4_ = bf16[128,2176]{1,0:T(8,128)(2,1)} collective-permute-done((bf16[128,2176]{1,0:T(8,128)(2,1)S(1)}, bf16[128,2176]{1,0:T(8,128)(2,1)}, u32[]{:S(2)}, u32[]{:S(2)}) %collective-permute-start.26) | collective-permute-done | bytes 557088 | tf_op jit(solution)/shard_map/ppermute | solution.py:261
  274.7 11.5 %collective-permute-done.34.refs_12_ = bf16[128,2176]{1,0:T(8,128)(2,1)S(1)} collective-permute-done((bf16[128,2176]{1,0:T(8,128)(2,1)S(1)}, bf16[128,2176]{1,0:T(8,128)(2,1)S(1)}, u32[]{:S(2)}, u32[]{:S(2)}) %collective-permute-start.34) | collective-permute-done | bytes 557088 | tf_op jit(solution)/shard_map/ppermute | solution.py:261
  288.3 11.6 %collective-permute-done.32.refs_10_ = bf16[128,2176]{1,0:T(8,128)(2,1)S(1)} collective-permute-done((bf16[128,2176]{1,0:T(8,128)(2,1)S(1)}, bf16[128,2176]{1,0:T(8,128)(2,1)S(1)}, u32[]{:S(2)}, u32[]{:S(2)}) %collective-permute-start.32) | collective-permute-done | bytes 557088 | tf_op jit(solution)/shard_map/ppermute | solution.py:261
  314.0 14.2 %dispatch.2 = (bf16[2048,2048]{1,0:T(8,128)(2,1)}, bf16[2048,128]{1,0:T(8,128)(2,1)S(1)}, bf16[1280,2048]{1,0:T(8,128)(2,1)}, f32[1280,1]{1,0:T(8,128)}) custom-call(s32[16]{0:T(128)S(1)} %fusion.60.base_ref, s32[16]{0:T(128)S(1)} %fusion.61.order_ref.to_ref, s32[16,1,128]{2,1,0:T(1,128)S(1)} %fusion.46.pos_ref, ...), custom_call_target="tpu_custom_call" | custom-call | tf_op jit(solution)/shard_map/dispatch/pallas_call | solution.py:415
  328.2 8.6 fusion.70
  337.0 14.6 %dispatch.3 = (bf16[1280,2048]{1,0:T(8,128)(2,1)}, f32[1280,1]{1,0:T(8,128)S(1)}) custom-call(s32[16]{0:T(128)S(1)} %fusion.60.base_ref, s32[16]{0:T(128)S(1)} %fusion.61.order_ref.to_ref, s32[16,1,128]{2,1,0:T(1,128)S(1)} %fusion.46.pos_ref, f32[16,1,128]{2,1,0:T(1,128)S(1)} %bitcast.216, bf16[2048,2048]{1,0:T(8,128)(2,1)} %all-gather.5.cloned.1.call-done.refs_0_), custom_call_target="tpu_custom_call" | custom-call | tf_op jit(solution)/shard_map/dispatch/pallas_call | solution.py:415
  351.6 8.4 multiply_convert_fusion.1
  360.0 16.4 %collective-permute-done.41.refs_6_ = bf16[352,2048]{1,0:T(8,128)(2,1)} collective-permute-done((bf16[352,2048]{1,0:T(8,128)(2,1)}, bf16[352,2048]{1,0:T(8,128)(2,1)}, u32[]{:S(2)}, u32[]{:S(2)}) %collective-permute-start.41) | collective-permute-done | bytes 1441824 | tf_op jit(solution)/shard_map/ppermute | solution.py:630
  376.4 63.3 %expert.1 = (bf16[1280,2048]{1,0:T(8,128)(2,1)}, bf16[1280,2048]{1,0:T(8,128)(2,1)}, bf16[1280,1408]{1,0:T(8,128)(2,1)}, bf16[1280,2048]{1,0:T(8,128)(2,1)}, bf1...) custom-call(s32[1]{0:T(128)} %bitcast.36.total_ref, s32[8]{0:T(128)} %stack.89.starts_ref, ...), custom_call_target="tpu_custom_call" | custom-call | tf_op jit(solution)/shard_map/expert/pallas_call | solution.py:498
  442.2 10.9 %combine.2 = bf16[2048,2048]{1,0:T(8,128)(2,1)} custom-call(s32[16]{0:T(128)S(1)} %fusion.60.base_ref, s32[16]{0:T(128)S(1)} %fusion.61.order_ref.to_ref, s32[16]{0:T(128)S(1)} %fusion.61.order_ref.to_ref, s32[1]{0:T(128)} %bitcast.33.me_ref, s32[16,1,128]{2,1,0:T(1,128)S(1)} %fusion.46.pos_ref, bf16[1280,2048]{1,0:T(8,128)(2,1)S(1)} %copy-done.3, ...), custom_call_target="tpu_custom_call" | custom-call | tf_op jit(solution)/shard_map/combine/pallas_call | solution.py:546
  458.3 14.0 %combine.3 = bf16[2048,2176]{1,0:T(8,128)(2,1)} custom-call(s32[16]{0:T(128)S(1)} %fusion.60.base_ref, s32[16]{0:T(128)S(1)} %fusion.61.order_ref.to_ref, s32[16]{0:T(128)S(1)} %iota.41.to_ref, s32[1]{0:T(128)} %bitcast.33.me_ref, s32[16,1,128]{2,1,0:T(1,128)S(1)} %fusion.46.pos_ref, bf16[1280,2048]{1,0:T(8,128)(2,1)S(1)} %copy-done.2, ...), custom_call_target="tpu_custom_call" | custom-call | tf_op jit(solution)/shard_map/combine/pallas_call | solution.py:546
  493.5 10.6 %convolution_bitcast_fusion = f32[1,1024,2816]{2,1,0:T(8,128)} fusion(bf16[1280,2816]{1,0:T(8,128)(2,1)S(1)} %bitcast.218, bf16[1280,2048]{1,0:T(8,128)(2,1)S(1)} %bitcast.227, s32[]{:T(128)S(6)} %select_n.235), kind=kOutput, calls=%fused_computation.3 | convolution fusion | flops 7381975040 | bytes 21364740 | tf_op jit(solution)/shard_map/dot_general | solution.py:54
  512.0 6.9 fusion.72
  519.0 14.4 %collective-permute-done.52 = bf16[128,2176]{1,0:T(8,128)(2,1)S(1)} collective-permute-done((bf16[128,2176]{1,0:T(8,128)(2,1)S(1)}, bf16[128,2176]{1,0:T(8,128)(2,1)S(1)}, u32[]{:S(2)}, u32[]{:S(2)}) %collective-permute-start.52) | collective-permute-done | bytes 557088 | tf_op jit(solution)/shard_map/ppermute | solution.py:261
  540.5 10.6 %collective-permute-done.53 = bf16[128,2176]{1,0:T(8,128)(2,1)S(1)} collective-permute-done((bf16[128,2176]{1,0:T(8,128)(2,1)S(1)}, bf16[128,2176]{1,0:T(8,128)(2,1)S(1)}, u32[]{:S(2)}, u32[]{:S(2)}) %collective-permute-start.53) | collective-permute-done | bytes 557088 | tf_op jit(solution)/shard_map/ppermute | solution.py:261
  554.4 18.1 %collective-permute-done.58 = bf16[64,2176]{1,0:T(8,128)(2,1)S(1)} collective-permute-done((bf16[64,2176]{1,0:T(8,128)(2,1)S(1)}, bf16[64,2176]{1,0:T(8,128)(2,1)S(1)}, u32[]{:S(2)}, u32[]{:S(2)}) %collective-permute-start.58) | collective-permute-done | bytes 278560 | tf_op jit(solution)/shard_map/ppermute | solution.py:261
  572.7 9.3 %convolution_bitcast_fusion.1 = f32[1,704,2048]{2,1,0:T(8,128)} fusion(bf16[1280,2048]{1,0:T(8,128)(2,1)} %get-tuple-element.37, bf16[1280,1408]{1,0:T(8,128)(2,1)S(1)} %copy-done.72, s32[]{:T(128)S(6)} %select_n.238), kind=kOutput, calls=%fused_computation.9 | convolution fusion | flops 3690987520 | bytes 12976132 | tf_op jit(solution)/shard_map/dot_general | solution.py:54
  594.1 7.2 collective-permute-done.60
  659.3 10.8 %attend_back.1 = bf16[2048,384]{1,0:T(8,128)(2,1)S(1)} custom-call(s32[16]{0:T(128)S(1)} %fusion.61.order_ref.to_ref, bf16[2048,128]{1,0:T(8,128)(2,1)S(1)} %copy-done.9, bf16[2048,128]{1,0:T(8,128)(2,1)S(1)} %copy-done.10, bf16[2048,128]{1,0:T(8,128)(2,1)S(1)} %copy-done.11, bf16[2048,128]{1,0:T(8,128)(2,1)S(1)} %bitcast.211, ...), custom_call_target="tpu_custom_call" | custom-call | tf_op jit(solution)/shard_map/attend_back/pallas_call | solution.py:201
  692.0 12.2 %collective-permute-done.72 = bf16[256,2816]{1,0:T(8,128)(2,1)} collective-permute-done((bf16[256,2816]{1,0:T(8,128)(2,1)}, bf16[256,2816]{1,0:T(8,128)(2,1)}, u32[]{:S(2)}, u32[]{:S(2)}) %collective-permute-start.72) | collective-permute-done | bytes 1441824 | tf_op jit(solution)/shard_map/ppermute | solution.py:759
  726.1 9.0 collective-permute-done.68
  767.1 7.2 collective-permute-start.71
  794.6 34.4 %collective-permute-done.77 = bf16[64,2048]{1,0:T(8,128)(2,1)S(1)} collective-permute-done((bf16[64,2048]{1,0:T(8,128)(2,1)S(1)}, bf16[64,2048]{1,0:T(8,128)(2,1)S(1)}, u32[]{:S(2)}, u32[]{:S(2)}) %collective-permute-start.77) | collective-permute-done | bytes 262176 | tf_op jit(solution)/shard_map/ppermute | solution.py:261
  834.9 13.7 %collective-permute-done.78 = bf16[128,2048]{1,0:T(8,128)(2,1)S(1)} collective-permute-done((bf16[128,2048]{1,0:T(8,128)(2,1)S(1)}, bf16[128,2048]{1,0:T(8,128)(2,1)S(1)}, u32[]{:S(2)}, u32[]{:S(2)}) %collective-permute-start.78) | collective-permute-done | bytes 524320 | tf_op jit(solution)/shard_map/ppermute | solution.py:261
  852.8 10.4 %collective-permute-done.79 = bf16[128,2048]{1,0:T(8,128)(2,1)S(1)} collective-permute-done((bf16[128,2048]{1,0:T(8,128)(2,1)S(1)}, bf16[128,2048]{1,0:T(8,128)(2,1)S(1)}, u32[]{:S(2)}, u32[]{:S(2)}) %collective-permute-start.79) | collective-permute-done | bytes 524320 | tf_op jit(solution)/shard_map/ppermute | solution.py:261
  (544 shorter events, 424.2 us)
Async XLA Ops:
  7.2 212.8 %all-gather.3.cloned.1.call-start = ((), (), s32[]{:S(2)}) async-start(), calls=%async_computation.8 | async-start | bytes 8912896 | tf_op jit(solution)/shard_map/all_gather | solution.py:569
  18.7 318.3 %all-gather.5.cloned.1.call-start = ((), (), s32[]{:S(2)}) async-start(), calls=%async_computation.9 | async-start | bytes 8912896 | tf_op jit(solution)/shard_map/all_gather | solution.py:569
  29.7 100.7 %collective-permute-start.20 = (bf16[256,2816]{1,0:T(8,128)(2,1)}, bf16[256,2816]{1,0:T(8,128)(2,1)}, u32[]{:S(2)}, u32[]{:S(2)}) collective-permute-start(bf16[256,2816]{1,0:T(8,128)(2,1)} %get-tuple-element.125), channel_id=1, source_target_pairs={{0,16},{16,0},{1,17},{17,1},{2,18},{18,2},{3,19},{19,3},{4,20},{20... | collective-permute-start | bytes 4325384 | tf_op jit(solution)/shard_map/ppermute | solution.py:630
  30.0 100.5 %collective-permute-start.19 = (bf16[256,2816]{1,0:T(8,128)(2,1)}, bf16[256,2816]{1,0:T(8,128)(2,1)}, u32[]{:S(2)}, u32[]{:S(2)}) collective-permute-start(bf16[256,2816]{1,0:T(8,128)(2,1)} %get-tuple-element.126), channel_id=1, source_target_pairs={{0,16},{16,0},{1,17},{17,1},{2,18},{18,2},{3,19},{19,3},{4,20},{20... | collective-permute-start | bytes 4325384 | tf_op jit(solution)/shard_map/ppermute | solution.py:630
  62.0 61.8 %collective-permute-start.4 = (bf16[128,2048]{1,0:T(8,128)(2,1)}, bf16[128,2048]{1,0:T(8,128)(2,1)}, u32[]{:S(2)}, u32[]{:S(2)}) collective-permute-start(bf16[128,2048]{1,0:T(8,128)(2,1)} %collective-permute-done.3.refs_4_), channel_id=1, source_target_pairs={{0,1},{1,0},{2,3},{3,2},{4,5},{5,4},{6,7},{7,6},{8,9},{9,8},{10,11... | collective-permute-start | bytes 1572872 | tf_op jit(solution)/shard_map/ppermute | solution.py:266
  83.9 40.0 %collective-permute-start.11 = (bf16[128,2048]{1,0:T(8,128)(2,1)}, bf16[128,2048]{1,0:T(8,128)(2,1)}, u32[]{:S(2)}, u32[]{:S(2)}) collective-permute-start(bf16[128,2048]{1,0:T(8,128)(2,1)} %multiply_convert_fusion.10), channel_id=1, source_target_pairs={{0,2},{1,3},{4,0},{5,1},{8,4},{9,5},{12,8},{13,9},{14,12},{15,13},... | collective-permute-start | bytes 1572872 | tf_op jit(solution)/shard_map/ppermute | solution.py:261
  138.3 63.9 %collective-permute-start.22 = (bf16[256,2816]{1,0:T(8,128)(2,1)}, bf16[256,2816]{1,0:T(8,128)(2,1)}, u32[]{:S(2)}, u32[]{:S(2)}) collective-permute-start(bf16[256,2816]{1,0:T(8,128)(2,1)} %get-tuple-element.124), channel_id=1, source_target_pairs={{0,16},{16,0},{1,17},{17,1},{2,18},{18,2},{3,19},{19,3},{4,20},{20... | collective-permute-start | bytes 4325384 | tf_op jit(solution)/shard_map/ppermute | solution.py:630
  159.4 70.2 %collective-permute-start.44 = (bf16[88,2048]{1,0:T(8,128)(2,1)}, bf16[88,2048]{1,0:T(8,128)(2,1)}, u32[]{:S(2)}, u32[]{:S(2)}) collective-permute-start(bf16[88,2048]{1,0:T(8,128)(2,1)} %param.22), channel_id=1, source_target_pairs={{0,16},{16,0},{1,17},{17,1},{2,18},{18,2},{3,19},{19,3},{4,20},{20... | collective-permute-start | bytes 1081352 | tf_op jit(solution)/shard_map/ppermute | solution.py:223
  159.5 87.3 %collective-permute-start.36 = (bf16[256,2816]{1,0:T(8,128)(2,1)}, bf16[256,2816]{1,0:T(8,128)(2,1)}, u32[]{:S(2)}, u32[]{:S(2)}) collective-permute-start(bf16[256,2816]{1,0:T(8,128)(2,1)} %get-tuple-element.123), channel_id=1, source_target_pairs={{0,16},{16,0},{1,17},{17,1},{2,18},{18,2},{3,19},{19,3},{4,20},{20... | collective-permute-start | bytes 4325384 | tf_op jit(solution)/shard_map/ppermute | solution.py:630
  218.8 398.0 %reduce-scatter.3.cloned.1.call-start = ((), (), s32[]{:S(2)}) async-start(), calls=%async_computation.10 | async-start | bytes 8912896 | tf_op jit(solution)/shard_map/reduce_scatter | solution.py:751
  251.7 48.3 %collective-permute-start.43 = (bf16[16,64,352]{2,1,0:T(8,128)(2,1)S(1)}, bf16[16,64,352]{2,1,0:T(8,128)(2,1)S(1)}, u32[]{:S(2)}, u32[]{:S(2)}) collective-permute-start(bf16[16,64,352]{2,1,0:T(8,128)(2,1)S(1)} %all-to-all-done.2), channel_id=1, source_target_pairs={{0,16},{16,0},{1,17},{17,1},{2,18},{18,2},{3,19},{19,3},{4,20},{20... | collective-permute-start | bytes 2162696 | tf_op jit(solution)/shard_map/ppermute | solution.py:223
  253.2 48.5 %collective-permute-start.23 = (bf16[128,2176]{1,0:T(8,128)(2,1)S(1)}, bf16[128,2176]{1,0:T(8,128)(2,1)S(1)}, u32[]{:S(2)}, u32[]{:S(2)}) collective-permute-start(bf16[128,2176]{1,0:T(8,128)(2,1)S(1)} %concatenate.54.refs_0_), channel_id=1, source_target_pairs={{0,1},{1,0},{2,3},{3,2},{4,5},{5,4},{6,7},{7,6},{8,9},{9,8},{10,11... | collective-permute-start | bytes 1671176 | tf_op jit(solution)/shard_map/ppermute | solution.py:266
  253.2 48.9 %collective-permute-start.27 = (bf16[128,2176]{1,0:T(8,128)(2,1)}, bf16[128,2176]{1,0:T(8,128)(2,1)S(1)}, u32[]{:S(2)}, u32[]{:S(2)}) collective-permute-start(bf16[128,2176]{1,0:T(8,128)(2,1)} %collective-permute-done.26.refs_4_), channel_id=1, source_target_pairs={{0,1},{1,0},{2,3},{3,2},{4,5},{5,4},{6,7},{7,6},{8,9},{9,8},{10,11... | collective-permute-start | bytes 1671176 | tf_op jit(solution)/shard_map/ppermute | solution.py:266
  311.1 48.9 %collective-permute-start.42 = (bf16[352,2048]{1,0:T(8,128)(2,1)}, bf16[352,2048]{1,0:T(8,128)(2,1)}, u32[]{:S(2)}, u32[]{:S(2)}) collective-permute-start(bf16[352,2048]{1,0:T(8,128)(2,1)} %get-tuple-element.130), channel_id=1, source_target_pairs={{0,16},{16,0},{1,17},{17,1},{2,18},{18,2},{3,19},{19,3},{4,20},{20... | collective-permute-start | bytes 4325384 | tf_op jit(solution)/shard_map/ppermute | solution.py:630
  311.7 64.6 %collective-permute-start.41 = (bf16[352,2048]{1,0:T(8,128)(2,1)}, bf16[352,2048]{1,0:T(8,128)(2,1)}, u32[]{:S(2)}, u32[]{:S(2)}) collective-permute-start(bf16[352,2048]{1,0:T(8,128)(2,1)} %get-tuple-element.131), channel_id=1, source_target_pairs={{0,16},{16,0},{1,17},{17,1},{2,18},{18,2},{3,19},{19,3},{4,20},{20... | collective-permute-start | bytes 4325384 | tf_op jit(solution)/shard_map/ppermute | solution.py:630
  482.7 122.9 %collective-permute-start.45 = (bf16[352,2048]{1,0:T(8,128)(2,1)}, bf16[352,2048]{1,0:T(8,128)(2,1)}, u32[]{:S(2)}, u32[]{:S(2)}) collective-permute-start(bf16[352,2048]{1,0:T(8,128)(2,1)} %convolution_convert_fusion.7), channel_id=1, source_target_pairs={{0,16},{16,0},{1,17},{17,1},{2,18},{18,2},{3,19},{19,3},{4,20},{20... | collective-permute-start | bytes 4325384 | tf_op jit(solution)/shard_map/ppermute | solution.py:759
  489.9 118.7 %collective-permute-start.62 = (bf16[352,2048]{1,0:T(8,128)(2,1)}, bf16[352,2048]{1,0:T(8,128)(2,1)S(1)}, u32[]{:S(2)}, u32[]{:S(2)}) collective-permute-start(bf16[352,2048]{1,0:T(8,128)(2,1)} %convolution_convert_fusion.6), channel_id=1, source_target_pairs={{0,16},{16,0},{1,17},{17,1},{2,18},{18,2},{3,19},{19,3},{4,20},{20... | collective-permute-start | bytes 4325384 | tf_op jit(solution)/shard_map/ppermute | solution.py:759
  491.3 48.7 %collective-permute-start.57 = (bf16[128,2176]{1,0:T(8,128)(2,1)}, bf16[128,2176]{1,0:T(8,128)(2,1)}, u32[]{:S(2)}, u32[]{:S(2)}) collective-permute-start(bf16[128,2176]{1,0:T(8,128)(2,1)} %get-tuple-element.100), channel_id=1, source_target_pairs={{0,1},{1,0},{2,3},{3,2},{4,5},{5,4},{6,7},{7,6},{8,9},{9,8},{10,11... | collective-permute-start | bytes 1671176 | tf_op jit(solution)/shard_map/ppermute | solution.py:266
  540.0 70.7 %collective-permute-start.46 = (bf16[128,2176]{1,0:T(8,128)(2,1)S(1)}, bf16[128,2176]{1,0:T(8,128)(2,1)S(1)}, u32[]{:S(2)}, u32[]{:S(2)}) collective-permute-start(bf16[128,2176]{1,0:T(8,128)(2,1)S(1)} %get-tuple-element.99), channel_id=1, source_target_pairs={{0,1},{1,0},{2,3},{3,2},{4,5},{5,4},{6,7},{7,6},{8,9},{9,8},{10,11... | collective-permute-start | bytes 1671176 | tf_op jit(solution)/shard_map/ppermute | solution.py:266
  540.0 42.1 %collective-permute-start.56 = (bf16[128,2176]{1,0:T(8,128)(2,1)}, bf16[128,2176]{1,0:T(8,128)(2,1)S(1)}, u32[]{:S(2)}, u32[]{:S(2)}) collective-permute-start(bf16[128,2176]{1,0:T(8,128)(2,1)} %get-tuple-element.101), channel_id=1, source_target_pairs={{0,1},{1,0},{2,3},{3,2},{4,5},{5,4},{6,7},{7,6},{8,9},{9,8},{10,11... | collective-permute-start | bytes 1671176 | tf_op jit(solution)/shard_map/ppermute | solution.py:266
  605.5 41.5 %collective-permute-start.83 = (bf16[16,64,352]{2,1,0:T(8,128)(2,1)}, bf16[16,64,352]{2,1,0:T(8,128)(2,1)}, u32[]{:S(2)}, u32[]{:S(2)}) collective-permute-start(bf16[16,64,352]{2,1,0:T(8,128)(2,1)} %fusion.29), channel_id=1, source_target_pairs={{0,16},{16,0},{1,17},{17,1},{2,18},{18,2},{3,19},{19,3},{4,20},{20... | collective-permute-start | bytes 2162696 | tf_op jit(solution)/shard_map/ppermute | solution.py:243
  608.7 77.5 %collective-permute-start.84 = (bf16[88,2048]{1,0:T(8,128)(2,1)}, bf16[88,2048]{1,0:T(8,128)(2,1)}, u32[]{:S(2)}, u32[]{:S(2)}) collective-permute-start(bf16[88,2048]{1,0:T(8,128)(2,1)} %fusion.37), channel_id=1, source_target_pairs={{0,16},{16,0},{1,17},{17,1},{2,18},{18,2},{3,19},{19,3},{4,20},{20... | collective-permute-start | bytes 1081352 | tf_op jit(solution)/shard_map/ppermute | solution.py:243
  637.9 52.3 %collective-permute-start.69 = (bf16[256,2816]{1,0:T(8,128)(2,1)}, bf16[256,2816]{1,0:T(8,128)(2,1)}, u32[]{:S(2)}, u32[]{:S(2)}) collective-permute-start(bf16[256,2816]{1,0:T(8,128)(2,1)} %convolution_convert_fusion.5), channel_id=1, source_target_pairs={{0,16},{16,0},{1,17},{17,1},{2,18},{18,2},{3,19},{19,3},{4,20},{20... | collective-permute-start | bytes 4325384 | tf_op jit(solution)/shard_map/ppermute | solution.py:759
  640.5 63.6 %collective-permute-start.72 = (bf16[256,2816]{1,0:T(8,128)(2,1)}, bf16[256,2816]{1,0:T(8,128)(2,1)}, u32[]{:S(2)}, u32[]{:S(2)}) collective-permute-start(bf16[256,2816]{1,0:T(8,128)(2,1)} %convolution_convert_fusion.4), channel_id=1, source_target_pairs={{0,16},{16,0},{1,17},{17,1},{2,18},{18,2},{3,19},{19,3},{4,20},{20... | collective-permute-start | bytes 4325384 | tf_op jit(solution)/shard_map/ppermute | solution.py:759
  649.3 56.6 %all-to-all-start.5 = ((bf16[16,64,352]{2,1,0:T(8,128)(2,1)}), bf16[16,64,352]{2,1,0:T(8,128)(2,1)}, u32[]{:S(2)}, u32[]{:S(2)}) async-start(bf16[16,64,352]{2,1,0:T(8,128)(2,1)} %fusion.13), calls=%async_computation.7 | async-start | bytes 1572864 | tf_op jit(solution)/shard_map/all_to_all | solution.py:573
  655.7 237.0 %reduce-scatter.5.cloned.1.call-start = ((), (), s32[]{:S(2)}) async-start(), calls=%async_computation.11 | async-start | bytes 8912896 | tf_op jit(solution)/shard_map/reduce_scatter | solution.py:814
  686.2 198.4 %collective-permute-start.85 = (bf16[256,2816]{1,0:T(8,128)(2,1)}, bf16[256,2816]{1,0:T(8,128)(2,1)}, u32[]{:S(2)}, u32[]{:S(2)}) collective-permute-start(bf16[256,2816]{1,0:T(8,128)(2,1)} %convolution_convert_fusion.3), channel_id=1, source_target_pairs={{0,16},{16,0},{1,17},{17,1},{2,18},{18,2},{3,19},{19,3},{4,20},{20... | collective-permute-start | bytes 4325384 | tf_op jit(solution)/shard_map/ppermute | solution.py:759
  780.1 108.5 %collective-permute-start.86 = (bf16[256,2816]{1,0:T(8,128)(2,1)}, bf16[256,2816]{1,0:T(8,128)(2,1)}, u32[]{:S(2)}, u32[]{:S(2)}) collective-permute-start(bf16[256,2816]{1,0:T(8,128)(2,1)} %convolution_convert_fusion.2), channel_id=1, source_target_pairs={{0,16},{16,0},{1,17},{17,1},{2,18},{18,2},{3,19},{19,3},{4,20},{20... | collective-permute-start | bytes 4325384 | tf_op jit(solution)/shard_map/ppermute | solution.py:759
  783.2 81.6 %all-to-all-start.4 = ((bf16[16,64,512]{2,1,0:T(8,128)(2,1)}), bf16[16,64,512]{2,1,0:T(8,128)(2,1)S(1)}, u32[]{:S(2)}, u32[]{:S(2)}) async-start(bf16[16,64,512]{2,1,0:T(8,128)(2,1)} %fusion.9), calls=%async_computation.5 | async-start | bytes 2097152 | tf_op jit(solution)/shard_map/all_to_all | solution.py:573
  789.2 87.9 %collective-permute-start.63 = (bf16[128,2048]{1,0:T(8,128)(2,1)}, bf16[128,2048]{1,0:T(8,128)(2,1)}, u32[]{:S(2)}, u32[]{:S(2)}) collective-permute-start(bf16[128,2048]{1,0:T(8,128)(2,1)} %get-tuple-element.111), channel_id=1, source_target_pairs={{0,1},{1,0},{2,3},{3,2},{4,5},{5,4},{6,7},{7,6},{8,9},{9,8},{10,11... | collective-permute-start | bytes 1572872 | tf_op jit(solution)/shard_map/ppermute | solution.py:266
  789.6 45.1 %collective-permute-start.75 = (bf16[128,2048]{1,0:T(8,128)(2,1)}, bf16[128,2048]{1,0:T(8,128)(2,1)S(1)}, u32[]{:S(2)}, u32[]{:S(2)}) collective-permute-start(bf16[128,2048]{1,0:T(8,128)(2,1)} %get-tuple-element.113), channel_id=1, source_target_pairs={{0,1},{1,0},{2,3},{3,2},{4,5},{5,4},{6,7},{7,6},{8,9},{9,8},{10,11... | collective-permute-start | bytes 1572872 | tf_op jit(solution)/shard_map/ppermute | solution.py:266
  789.8 39.3 %collective-permute-start.77 = (bf16[64,2048]{1,0:T(8,128)(2,1)S(1)}, bf16[64,2048]{1,0:T(8,128)(2,1)S(1)}, u32[]{:S(2)}, u32[]{:S(2)}) collective-permute-start(bf16[64,2048]{1,0:T(8,128)(2,1)S(1)} %copy-done.63), channel_id=1, source_target_pairs={{0,2},{1,3},{4,0},{5,1},{8,4},{9,5},{12,8},{13,9},{14,12},{15,13},... | collective-permute-start | bytes 786440 | tf_op jit(solution)/shard_map/ppermute | solution.py:261
  (151 other events, 2328.9 us)
Sparse Core Ops, SparseCore 0:
  18.8 102.3 all-gather.2
  123.3 80.1 all-gather.4
  453.3 125.7 reduce-scatter.2
  686.3 140.5 reduce-scatter.4
